TPU v7x, 32 devices: a whole 2x2x4 slice. The times are simulated.
32 devices in a mesh: groups: 2 (over y), ctx: 4 (over z), section: 2 (over x), head: 2 (over core).
Axes of the slice: x: 2, y: 2, z: 4, core: 2. Of those that a mesh axis runs over, the one named last changes fastest.
Arguments:
- queries: bfloat16 [2, 2, 2048, 3584], P('section', None, ('groups', 'ctx'), 'head'), parts along dimension 2, may hold values from -120 to 120
- key_row_table: bfloat16 [2, 2, 2048, 512], P('section', None, ('groups', 'ctx'), 'head'), parts along dimension 2, may hold values from -7 to 7
- value_row_table: bfloat16 [2, 2, 2048, 512], P('section', None, ('groups', 'ctx'), 'head'), parts along dimension 2, may hold values from -6 to 6
- vertical_cols: int32 [2, 4, 2048], P('section', 'head', 'groups'), parts along dimension 2, may hold values from 0 to 2047, as said below
- slash_offsets: int32 [2, 28, 128], P('section', 'head', 'groups'), parts along dimension 2, may hold values from 0 to 255, as said below
Outputs:
- attended: bfloat16 [2, 2, 2048, 3584], P('section', None, ('groups', 'ctx'), 'head'), parts along dimension 2
There are 2 independent parts, one for each index of `groups`. A program takes and returns all parts, laid end to end along the dimension named above; each array names one. Nothing has to cross between parts.
Inputs may be any that keep to these rules, and one draw needn't show every extreme that they name: `vertical_cols`: each run of 128 entries of a kv head's list (a tile) holds positions of one rank's rows of one micro-half; a kv head's positions are distinct; at most 2 tiles of a kv head lie on one rank, and for every kv head some rank holds exactly 2. `slash_offsets`: each head's offsets are distinct and include 0 and 255.
All inputs are finite; a program needn't handle non-finite values.
Results may differ from a plain program's by a relative error of at most 0.0032.
Values may be sent and summed in bfloat16 or wider, within the bound.
No kernel may reach another device: no remote copies, remote signals or barrier semaphores. Data moves between devices by JAX's collectives and lax.ppermute only.
A program may use at most 64 MiB of HBM per device.

v0:
```python
import jax
import jax.numpy as jnp
from jax import lax
from jax.sharding import PartitionSpec as P

HEAD_SIZE = 128
TILE_COLUMNS = 128
MAXT = 2


def passed_along(x, axis, by):
    length = lax.axis_size(axis)
    return lax.ppermute(x, axis, [(i, (i + by) % length) for i in range(length)])


def band_table(offsets, row_count):
    offset_hit = jnp.any(
        jnp.arange(row_count, dtype=jnp.int32)[:, None] == offsets[None, :], axis=1
    )
    padded = jnp.concatenate(
        [jnp.zeros((1,), jnp.bool_), offset_hit[::-1], jnp.zeros((2 * row_count - 1,), jnp.bool_)]
    )
    length = 3 * row_count
    repeated = jnp.tile(padded, row_count)[: row_count * (length - 1)]
    return repeated.reshape(row_count, length - 1)[:, : 2 * row_count]


def per_device(queries, key_row_table, value_row_table, vertical_cols, slash_offsets):
    rank_count = lax.axis_size("ctx")
    rank_id = lax.axis_index("ctx")
    row_count = queries.shape[2]
    kv_local = key_row_table.shape[3] // HEAD_SIZE
    q_local = queries.shape[3] // HEAD_SIZE
    group_size = q_local // kv_local
    half_len = row_count * rank_count
    scaling = 1.0 / HEAD_SIZE**0.5
    stacked = jnp.concatenate(
        [
            key_row_table[0].reshape(2, row_count, kv_local, HEAD_SIZE),
            value_row_table[0].reshape(2, row_count, kv_local, HEAD_SIZE),
        ],
        axis=3,
    )
    previous = passed_along(stacked, "ctx", 1)
    previous = jnp.where(rank_id == 0, previous[::-1], previous)
    band_kv = jnp.concatenate([previous, stacked], axis=1)
    halves = jnp.arange(2, dtype=jnp.int32)[:, None] * half_len
    band_pos = (
        halves
        + rank_id * row_count
        - row_count
        + jnp.arange(2 * row_count, dtype=jnp.int32)[None, :]
    )
    query_pos = halves + rank_id * row_count + jnp.arange(row_count, dtype=jnp.int32)[None, :]
    columns = vertical_cols[0]
    source_half = columns // half_len
    owners = columns % half_len // row_count
    source_row = columns % row_count
    picked = stacked[source_half, source_row, jnp.arange(kv_local, dtype=jnp.int32)[:, None]]
    tile_count = columns.shape[1] // TILE_COLUMNS
    tile_owner = owners.reshape(kv_local, tile_count, TILE_COLUMNS)[:, :, 0]
    tile_ids = jnp.arange(tile_count, dtype=jnp.int32)
    earlier = (tile_owner[:, None, :] == tile_owner[:, :, None]) & (
        tile_ids[None, :] < tile_ids[:, None]
    )[None]
    slot_rank = jnp.sum(earlier.astype(jnp.int32), axis=2)
    slot_ids = jnp.arange(MAXT, dtype=jnp.int32)
    selector = (
        (tile_owner[:, None, :] == rank_id) & (slot_rank[:, None, :] == slot_ids[None, :, None])
    ).astype(jnp.bfloat16)
    tile_rows = picked.reshape(kv_local, tile_count, TILE_COLUMNS * 2 * HEAD_SIZE)
    outbox = jnp.einsum(
        "gst,gtc->gsc", selector, tile_rows, preferred_element_type=jnp.float32
    ).astype(jnp.bfloat16)
    arrived = lax.all_gather(outbox, "ctx", axis=1, tiled=True)
    slot_index = tile_owner * MAXT + slot_rank
    vert_kv = arrived[jnp.arange(kv_local, dtype=jnp.int32)[:, None], slot_index].reshape(
        kv_local, tile_count * TILE_COLUMNS, 2 * HEAD_SIZE
    )
    marked = jnp.any(band_pos[None, :, :, None] == columns[:, None, None, :], axis=3)
    query_all = queries[0]
    offsets_all = slash_offsets[0]

    def one_head(head_id, result):
        group_id = head_id // group_size
        query_head = lax.dynamic_slice_in_dim(query_all, head_id * HEAD_SIZE, HEAD_SIZE, axis=2)
        vert_head = lax.dynamic_index_in_dim(vert_kv, group_id, 0, keepdims=False)
        band_head = lax.dynamic_index_in_dim(band_kv, group_id, 2, keepdims=False)
        cols_head = lax.dynamic_index_in_dim(columns, group_id, 0, keepdims=False)
        marked_head = lax.dynamic_index_in_dim(marked, group_id, 0, keepdims=False)
        offsets = lax.dynamic_index_in_dim(offsets_all, head_id, 0, keepdims=False)
        score_vert = (
            jnp.einsum(
                "mid,nd->min",
                query_head,
                vert_head[:, :HEAD_SIZE],
                preferred_element_type=jnp.float32,
            )
            * scaling
        )
        live_vert = cols_head[None, None, :] <= query_pos[:, :, None]
        score_band = (
            jnp.einsum(
                "mid,mjd->mij",
                query_head,
                band_head[:, :, :HEAD_SIZE],
                preferred_element_type=jnp.float32,
            )
            * scaling
        )
        live_band = (
            band_table(offsets, row_count)[None]
            & (band_pos >= 0)[:, None, :]
            & ~marked_head[:, None, :]
        )
        row_max = jnp.maximum(
            jnp.max(jnp.where(live_vert, score_vert, -jnp.inf), axis=2),
            jnp.max(jnp.where(live_band, score_band, -jnp.inf), axis=2),
        )
        expo_vert = jnp.exp(jnp.where(live_vert, score_vert - row_max[:, :, None], -jnp.inf))
        expo_band = jnp.exp(jnp.where(live_band, score_band - row_max[:, :, None], -jnp.inf))
        weight_sum = jnp.sum(expo_vert, axis=2) + jnp.sum(expo_band, axis=2)
        weighted = jnp.einsum(
            "min,nd->mid",
            expo_vert.astype(jnp.bfloat16),
            vert_head[:, HEAD_SIZE:],
            preferred_element_type=jnp.float32,
        )
        weighted = weighted + jnp.einsum(
            "mij,mjd->mid",
            expo_band.astype(jnp.bfloat16),
            band_head[:, :, HEAD_SIZE:],
            preferred_element_type=jnp.float32,
        )
        attended = (weighted / weight_sum[:, :, None]).astype(jnp.bfloat16)
        return lax.dynamic_update_slice_in_dim(result, attended, head_id * HEAD_SIZE, axis=2)

    result = lax.fori_loop(
        0, q_local, one_head, jnp.zeros((2, row_count, q_local * HEAD_SIZE), jnp.bfloat16)
    )
    return result[None]


def solution(mesh):
    in_specs = (
        P("section", None, ("groups", "ctx"), "head"),
        P("section", None, ("groups", "ctx"), "head"),
        P("section", None, ("groups", "ctx"), "head"),
        P("section", "head", "groups"),
        P("section", "head", "groups"),
    )
    out_specs = P("section", None, ("groups", "ctx"), "head")
    return jax.shard_map(
        per_device, mesh=mesh, in_specs=in_specs, out_specs=out_specs, check_vma=False
    )
```

profile of v0, /device:TPU:0, one launch (start us, length us, event | category | flops | bytes accessed | tf_op | source)
XLA Modules:
  0.0 181.4 jit_solution(9748537324119592758)
XLA Ops:
  8.4 1.0 reshape_squeeze.6
  9.6 1.0 reshape_squeeze.7
  11.0 13.0 %gather_fusion = bf16[2048,256]{1,0:T(8,128)(2,1)S(1)} fusion(bf16[2,256,2,256]{3,2,1,0:T(2,128)(2,1)S(1)} %constant_dynamic-update-slice_fusion, s32[2048]{0:T(1024)S(1)} %bitcast.75), kind=kCustom, calls=%fused_computation | custom fusion | bytes 2121728 | tf_op jit(solution)/shard_map/gather | solution.py:59
  25.0 1.0 copy.15
  26.0 3.3 %collective-permute-start = (bf16[2,256,2,256]{3,2,1,0:T(2,128)(2,1)S(1)}, bf16[2,256,2,256]{3,2,1,0:T(2,128)(2,1)S(1)}, u32[]{:S(2)}, u32[]{:S(2)}) collective-permute-start(bf16[2,256,2,256]{3,2,1,0:T(2,128)(2,1)S(1)} %constant_dynamic-update-slice_fusion), channel_id=1, source_target_pairs={{0,4},{4,8},{8,12},{12,0},{1,5},{5,9},{9,13},{13,1},{2,6},{6,10},{... | collective-permute-start | bytes 1572872 | tf_op jit(solution)/shard_map/ppermute | solution.py:13
  29.7 1.1 compare_reduce_fusion
  30.8 15.5 %collective-permute-done = bf16[2,256,2,256]{3,2,1,0:T(2,128)(2,1)S(1)} collective-permute-done((bf16[2,256,2,256]{3,2,1,0:T(2,128)(2,1)S(1)}, bf16[2,256,2,256]{3,2,1,0:T(2,128)(2,1)S(1)}, u32[]{:S(2)}, u32[]{:S(2)}) %collective-permute-start) | collective-permute-done | bytes 524320 | tf_op jit(solution)/shard_map/ppermute | solution.py:13
  46.7 1.4 pad_maximum_fusion
  48.2 12.3 %all-gather.2.cloned.1.call-done = bf16[2,8,32768]{2,0,1:T(2,128)(2,1)} async-done(((bf16[2,2,32768]{2,0,1:T(2,128)(2,1)}), bf16[2,8,32768]{2,0,1:T(2,128)(2,1)}) %all-gather.2.cloned.1.call-update) | async-done | bytes 1048592 | tf_op jit(solution)/shard_map/all_gather | solution.py:75
  60.5 1.8 copy.17
  62.3 3.6 %gather_fusion.1 = bf16[16,32768]{1,0:T(8,128)(2,1)S(1)} fusion(bf16[2,8,32768]{2,1,0:T(8,128)(2,1)S(1)} %copy.17, s32[16]{0:T(128)S(1)} %reshape.258), kind=kCustom, calls=%fused_computation.1 | custom fusion | bytes 2097280 | tf_op jit(solution)/shard_map/gather | solution.py:77
  66.4 1.3 broadcast_in_dim.80
  67.7 106.8 %while.16 = (s32[]{:T(128)}, bf16[2,256,1792]{2,1,0:T(8,128)(2,1)}, s32[2,1024]{1,0:T(2,128)S(1)}, bf16[2,256,1792]{2,1,0:T(8,128)(2,1)}, bf16[2,1024,256]{2,1,0...) while((s32[]{:T(128)}, bf16[2,256,1792]{2,1,0:T(8,128)(2,1)}, ...), condition=%wide.region_8.9_spmd.clone, body=%wide.region_2.8_spmd.clone.sunk | while | flops 414158592 | bytes 15215747 | solution.py:138
  68.6 0.8 reshape.272
  69.6 1.4 select_reduce_fusion.2
  71.0 1.5 fusion.68
  74.2 1.2 fusion.74
  76.3 0.8 reshape.272
  77.2 1.4 select_reduce_fusion.2
  78.6 1.5 fusion.68
  81.8 1.2 fusion.74
  83.9 0.8 reshape.272
  84.9 1.4 select_reduce_fusion.2
  86.2 1.5 fusion.68
  89.5 1.2 fusion.74
  91.5 0.8 reshape.272
  92.5 1.4 select_reduce_fusion.2
  93.8 1.5 fusion.68
  97.1 1.2 fusion.74
  99.1 0.8 reshape.272
  100.1 1.4 select_reduce_fusion.2
  101.5 1.5 fusion.68
  104.7 1.2 fusion.74
  106.8 0.8 reshape.272
  107.7 1.4 select_reduce_fusion.2
  109.1 1.5 fusion.68
  112.3 1.2 fusion.74
  115.4 1.4 select_reduce_fusion.2
  116.7 1.5 fusion.68
  120.0 1.2 fusion.74
  122.0 0.8 reshape.272
  123.0 1.4 select_reduce_fusion.2
  124.4 1.5 fusion.68
  127.6 1.2 fusion.74
  129.7 0.8 reshape.272
  130.6 1.4 select_reduce_fusion.2
  132.0 1.5 fusion.68
  135.2 1.2 fusion.74
  138.3 1.4 select_reduce_fusion.2
  139.6 1.5 fusion.68
  142.9 1.2 fusion.74
  144.9 0.8 reshape.272
  145.9 1.4 select_reduce_fusion.2
  147.3 1.5 fusion.68
  150.5 1.2 fusion.74
  153.5 1.4 select_reduce_fusion.2
  154.9 1.5 fusion.68
  158.1 1.2 fusion.74
  161.2 1.4 select_reduce_fusion.2
  162.5 1.5 fusion.68
  165.7 1.2 fusion.74
  168.8 1.4 select_reduce_fusion.2
  170.1 1.5 fusion.68
  173.4 1.2 fusion.74
  (298 shorter events, 47.4 us)
Async XLA Ops:
  6.5 53.9 %all-gather.2.cloned.1.call-start = ((), (), s32[]{:S(2)}) async-start(), calls=%async_computation | async-start | bytes 1310720 | tf_op jit(solution)/shard_map/all_gather | solution.py:75
  24.0 5.3 %copy-start.1 = (s32[1,14,64]{2,0,1:T(1,128)S(1)}, s32[1,14,64]{2,0,1:T(1,128)}, u32[]{:S(2)}) copy-start(s32[1,14,64]{2,0,1:T(1,128)} %param.11) | copy-start | bytes 10756
  24.0 5.7 %copy-start = (s32[1,2,1024]{2,1,0:T(2,128)S(1)}, s32[1,2,1024]{2,1,0:T(2,128)}, u32[]{:S(2)}) copy-start(s32[1,2,1024]{2,1,0:T(2,128)} %param.10) | copy-start | bytes 24580
  26.0 20.3 %collective-permute-start = (bf16[2,256,2,256]{3,2,1,0:T(2,128)(2,1)S(1)}, bf16[2,256,2,256]{3,2,1,0:T(2,128)(2,1)S(1)}, u32[]{:S(2)}, u32[]{:S(2)}) collective-permute-start(bf16[2,256,2,256]{3,2,1,0:T(2,128)(2,1)S(1)} %constant_dynamic-update-slice_fusion), channel_id=1, source_target_pairs={{0,4},{4,8},{8,12},{12,0},{1,5},{5,9},{9,13},{13,1},{2,6},{6,10},{... | collective-permute-start | bytes 1572872 | tf_op jit(solution)/shard_map/ppermute | solution.py:13
Sparse Core Ops, SparseCore 0:
  26.1 34.3 all-gather.1
where the time goes:
time: 182 us; the launch traced here: 181 us
  matrix products  65.2 us (36%)
  local copies, waits for them, and re-layouts  45.5 us (25%)
  waiting for transfers between devices  27.8 us (15%)
  other arithmetic  25.3 us (14%)
  between operations  13.5 us (7%)
  starting transfers between devices  3.26 us (2%)
    dot_general x14, matrix products, one_head(): jnp.einsum('mid,nd->min', query_head, vert_head[:, :HEAD_SIZE], preferred...  20.4 us
    dot_general x14, matrix products, one_head(): jnp.einsum('mid,mjd->mij', query_head, band_head[:, :, :HEAD_SIZE], prefe...  19 us
    dot_general x14, matrix products, one_head(): jnp.einsum('mij,mjd->mid', expo_band.astype(jnp.bfloat16), band_head[:, :...  16.4 us
    reduce_sum x28, other arithmetic, one_head(): weight_sum = jnp.sum(expo_vert, axis=2) + jnp.sum(expo_band, axis=2)  15.5 us
    ppermute x1, waiting for transfers between devices, passed_along(): lax.ppermute(x, axis, [(i, (i + by) % length) for i in range(length)])  15.5 us
    gather x1, local copies, waits for them, and re-layouts, per_device(): stacked[source_half, source_row, jnp.arange(kv_local, dtype=jnp.int32)[:,...  13 us
    all_gather x1, waiting for transfers between devices, per_device(): arrived = lax.all_gather(outbox, 'ctx', axis=1, tiled=True)  12.3 us
    reshape x14, local copies, waits for them, and re-layouts, band_table(): return repeated.reshape(row_count, length - 1)[:, :2 * row_count]  11.9 us
  transfers between devices with their start and end apart: 2, of which 2 were waited for; matrix products, arithmetic and copies ran while one was open for 2% of the time, Pallas kernels for 0%

commit v1 on v0

v1 whole, which is shorter than its diff:
```python
import functools
import math

import jax
import jax.numpy as jnp
from jax import lax
from jax.experimental import pallas as pl
from jax.experimental.pallas import tpu as pltpu
from jax.sharding import PartitionSpec as P

HEAD_SIZE = 128
TILE_COLUMNS = 128
MAXT = 2
DEAD = -1e30
SCALE2 = math.log2(math.e) / math.sqrt(HEAD_SIZE)
VMEM_BYTES = 48 * 1024 * 1024


def dot_nt(a, b):
    return lax.dot_general(a, b, (((1,), (1,)), ((), ())), preferred_element_type=jnp.float32)


def dot_nn(a, b):
    return lax.dot_general(a, b, (((1,), (0,)), ((), ())), preferred_element_type=jnp.float32)


def prep_kernel(n, rows, kv, rank_ref, cols_smem, cols_ref, k_ref, v_ref, *outs):
    pack0_ref, pack1_ref = outs[:2]
    payload_refs = outs[2 : 2 + n - 2]
    band_bias_ref, extra_bias_ref, remote_bias_ref = outs[2 + n - 2 : 5 + n - 2]
    outbox_ref, marks_ref, slot_ref, count_ref = outs[5 + n - 2 :]
    rank = rank_ref[0]
    half_len = rows * n
    tiles = cols_ref.shape[1] // TILE_COLUMNS
    per_rank = rows // TILE_COLUMNS
    pack0_ref[0] = k_ref[0]
    pack0_ref[1] = v_ref[0]
    pack1_ref[0] = k_ref[1]
    pack1_ref[1] = v_ref[1]

    for g in range(kv):
        for s in range(n):
            count_ref[g, s] = 0
            for slot in range(MAXT):
                slot_ref[g, s * MAXT + slot] = -1
        for t in range(tiles):
            owner = cols_smem[g, t * TILE_COLUMNS] % half_len // rows
            seen = count_ref[g, owner]
            slot_ref[g, owner * MAXT + seen] = t
            count_ref[g, owner] = seen + 1

    for g in range(kv):
        lanes = slice(g * HEAD_SIZE, (g + 1) * HEAD_SIZE)
        for slot in range(MAXT):
            tile = jnp.maximum(slot_ref[g, rank * MAXT + slot], 0)
            start = pl.multiple_of(tile * TILE_COLUMNS, TILE_COLUMNS)
            half = cols_smem[g, start] // half_len
            within = cols_ref[pl.ds(g, 1), pl.ds(start, TILE_COLUMNS)] % rows
            hit = lax.broadcasted_iota(jnp.int32, (rows, TILE_COLUMNS), 0) == within
            pick = jnp.where(hit, 1.0, 0.0).astype(jnp.bfloat16)
            for which, ref in enumerate((k_ref, v_ref)):
                source = ref[pl.ds(half, 1), :, lanes][0]
                got = lax.dot_general(
                    pick, source, (((0,), (0,)), ((), ())), preferred_element_type=jnp.float32
                )
                outbox_ref[which, slot * TILE_COLUMNS : (slot + 1) * TILE_COLUMNS, lanes] = (
                    got.astype(jnp.bfloat16)
                )
    for i, ref in enumerate(payload_refs):
        d = i + 2

        @pl.when(rank + d < n)
        def _():
            ref[...] = outbox_ref[...]

        @pl.when(rank + d >= n)
        def _():
            ref[0] = k_ref[0]
            ref[1] = v_ref[0]

    blocks = 2 * n * per_rank
    dead_row = jnp.full((1, rows), DEAD, jnp.float32)
    for g in range(kv):
        cols = cols_ref[g : g + 1, :]
        high = lax.broadcasted_iota(jnp.int32, (blocks, cols.shape[1]), 0) == cols // TILE_COLUMNS
        low = lax.broadcasted_iota(jnp.int32, (TILE_COLUMNS, cols.shape[1]), 0) == cols % TILE_COLUMNS
        count = dot_nt(
            jnp.where(high, 1.0, 0.0).astype(jnp.bfloat16),
            jnp.where(low, 1.0, 0.0).astype(jnp.bfloat16),
        )
        marks_ref[g] = jnp.where(count > 0.5, 0.0, DEAD)

        def marks_of(half, s):
            first = (half * n + s) * per_rank
            return jnp.concatenate(
                [marks_ref[g, pl.ds(first + i, 1), :] for i in range(per_rank)], axis=1
            )

        first_rank = rank == 0
        before = jnp.where(first_rank, n - 1, rank - 1)
        before_low = marks_of(0, before)
        own_low = marks_of(0, rank)
        own_high = marks_of(1, rank)
        before_high = marks_of(jnp.where(first_rank, 0, 1), before)
        band_bias_ref[g, 0:1, :rows] = jnp.where(first_rank, dead_row, before_low)
        band_bias_ref[g, 0:1, rows:] = own_low
        band_bias_ref[g, 1:2, :rows] = before_high
        band_bias_ref[g, 1:2, rows:] = own_high
        extra_bias_ref[g, 0:1, :rows] = own_low
        extra_bias_ref[g, 0:1, rows:] = jnp.where(first_rank, dead_row, before_low)
        for i in range(n - 2):
            d = i + 2
            earlier = rank >= d
            s = jnp.where(earlier, rank - d, rank - d + n)
            raw = marks_of(0, s)
            for slot in range(MAXT):
                tile = slot_ref[g, s * MAXT + slot]
                half = cols_smem[g, jnp.maximum(tile, 0) * TILE_COLUMNS] // half_len
                live = tile >= 0
                high_value = jnp.where(live, 0.0, DEAD)
                low_value = jnp.where(live & (half == 0) & earlier, 0.0, DEAD)
                span = slice(i * rows + slot * TILE_COLUMNS, i * rows + (slot + 1) * TILE_COLUMNS)
                part = slice(slot * TILE_COLUMNS, (slot + 1) * TILE_COLUMNS)
                remote_bias_ref[g, 0:1, span] = jnp.full((1, TILE_COLUMNS), low_value, jnp.float32)
                remote_bias_ref[g, 1:2, span] = jnp.where(
                    earlier, jnp.full((1, TILE_COLUMNS), high_value, jnp.float32), raw[:, part]
                )


def near_kernel(
    rows, kv, group_size,
    rank_ref, q_ref, k_ref, v_ref, in0_ref, in1_ref, band_bias_ref, extra_bias_ref, slash_ref,
    acc_ref, stat_ref,
    kb_ref, vb_ref, kx_ref, vx_ref, tri_ref,
):
    first_rank = rank_ref[0] == 0
    t = rows // 2
    tri = lax.broadcasted_iota(jnp.int32, (t, t), 0) >= lax.broadcasted_iota(jnp.int32, (t, t), 1)
    ones = jnp.ones((2 * rows, HEAD_SIZE), jnp.bfloat16)
    for g in range(kv):
        lanes = slice(g * HEAD_SIZE, (g + 1) * HEAD_SIZE)
        for which, own, band, extra in ((0, k_ref, kb_ref, kx_ref), (1, v_ref, vb_ref, vx_ref)):
            low = in0_ref[which, :, lanes]
            high = in1_ref[which, :, lanes]
            band[g, 0, :rows, :HEAD_SIZE] = low
            band[g, 0, rows:, :HEAD_SIZE] = own[0, :, lanes]
            band[g, 1, :rows, :HEAD_SIZE] = jnp.where(first_rank, low, high)
            band[g, 1, rows:, :HEAD_SIZE] = own[1, :, lanes]
            extra[g, :rows, :HEAD_SIZE] = own[0, :, lanes]
            extra[g, rows:, :HEAD_SIZE] = low
        for m in range(2):
            vb_ref[g, m, :, HEAD_SIZE:] = ones
            for b in range(2):
                row = band_bias_ref[g, m : m + 1, rows + b * t : rows + (b + 1) * t]
                tri_ref[g, m, b] = jnp.where(tri, row, DEAD)
        vx_ref[g, :, HEAD_SIZE:] = ones
    shut = jnp.where(first_rank, DEAD, 0.0)
    lane = lax.broadcasted_iota(jnp.int32, (rows, HEAD_SIZE), 1)

    for g in range(kv):

        def one_head(h, carry):
            head = g * group_size + h
            at = pl.ds(pl.multiple_of(head * HEAD_SIZE, HEAD_SIZE), HEAD_SIZE)
            base = jnp.broadcast_to(slash_ref[head], (t, 2 * rows))
            rolled = pltpu.roll(base, 1, 1, stride=1, stride_axis=0)
            t2, t1, t0 = rolled[:, :t], rolled[:, t : 2 * t], rolled[:, 2 * t : 3 * t]
            for m in range(2):
                q = q_ref[m, :, at]
                s = dot_nt(q, kb_ref[g, m]) * SCALE2
                p2, p1 = (t2 + shut, t1 + shut) if m == 0 else (t2, t1)
                row = [band_bias_ref[g, m : m + 1, b * t : (b + 1) * t] for b in range(4)]
                top = [
                    s[:t, :t] + jnp.maximum(p2, row[0]),
                    s[:t, t : 2 * t] + jnp.maximum(p1, row[1]),
                    s[:t, 2 * t : 3 * t] + jnp.maximum(t0, tri_ref[g, m, 0]),
                ]
                low = [
                    s[t:, :t] + row[0],
                    s[t:, t : 2 * t] + jnp.maximum(p2, row[1]),
                    s[t:, 2 * t : 3 * t] + jnp.maximum(t1, row[2]),
                    s[t:, 3 * t :] + jnp.maximum(t0, tri_ref[g, m, 1]),
                ]
                top_max = functools.reduce(jnp.maximum, top)
                low_max = functools.reduce(jnp.maximum, low)
                all_max = jnp.concatenate([top_max, low_max], axis=0)
                if m == 1:
                    sx = dot_nt(q, kx_ref[g]) * SCALE2 + extra_bias_ref[g]
                    for b in range(4):
                        all_max = jnp.maximum(all_max, sx[:, b * t : (b + 1) * t])
                peak = jnp.max(all_max, axis=1, keepdims=True)
                top = [jnp.exp2(x - peak[:t]).astype(jnp.bfloat16) for x in top]
                top.append(jnp.zeros((t, t), jnp.bfloat16))
                low = [jnp.exp2(x - peak[t:]).astype(jnp.bfloat16) for x in low]
                p = jnp.concatenate(
                    [jnp.concatenate(top, axis=1), jnp.concatenate(low, axis=1)], axis=0
                )
                o = dot_nn(p, vb_ref[g, m])
                if m == 1:
                    px = jnp.exp2(sx - peak).astype(jnp.bfloat16)
                    o = o + dot_nn(px, vx_ref[g])
                acc_ref[m, :, at] = o[:, :HEAD_SIZE]
                stat_ref[m, :, at] = jnp.where(lane < HEAD_SIZE // 2, peak, o[:, HEAD_SIZE:])
            return carry

        lax.fori_loop(0, group_size, one_head, 0)


def far_kernel(rows, kv, group_size, count, *refs):
    q_ref, acc_ref, stat_ref, remote_bias_ref = refs[:4]
    arrived = refs[4 : 4 + count]
    out_ref, kr_ref, vr_ref = refs[4 + count :]
    ones = jnp.ones((rows, HEAD_SIZE), jnp.bfloat16)
    for g in range(kv):
        lanes = slice(g * HEAD_SIZE, (g + 1) * HEAD_SIZE)
        for i, ref in enumerate(arrived):
            at = slice(i * rows, (i + 1) * rows)
            kr_ref[g, at, :] = ref[0, :, lanes]
            vr_ref[g, at, :HEAD_SIZE] = ref[1, :, lanes]
            vr_ref[g, at, HEAD_SIZE:] = ones

    for g in range(kv):

        def one_head(h, carry):
            head = g * group_size + h
            at = pl.ds(pl.multiple_of(head * HEAD_SIZE, HEAD_SIZE), HEAD_SIZE)
            for m in range(2):
                q = q_ref[m, :, at]
                s = dot_nt(q, kr_ref[g]) * SCALE2 + remote_bias_ref[g, m : m + 1, :]
                stat = stat_ref[m, :, at]
                old = stat[:, :1]
                peak = jnp.maximum(old, jnp.max(s, axis=1, keepdims=True))
                p = jnp.exp2(s - peak).astype(jnp.bfloat16)
                o = dot_nn(p, vr_ref[g])
                shrink = jnp.exp2(old - peak)
                total = stat[:, HEAD_SIZE - 1 :] * shrink + o[:, HEAD_SIZE:]
                out = (acc_ref[m, :, at] * shrink + o[:, :HEAD_SIZE]) / total
                out_ref[m, :, at] = out.astype(jnp.bfloat16)
            return carry

        lax.fori_loop(0, group_size, one_head, 0)


def per_device(queries, key_row_table, value_row_table, vertical_cols, slash_offsets):
    n = lax.axis_size("ctx")
    rank = lax.axis_index("ctx").astype(jnp.int32)
    rows = queries.shape[2]
    kv = key_row_table.shape[3] // HEAD_SIZE
    heads = queries.shape[3] // HEAD_SIZE
    group_size = heads // kv
    q, k, v = queries[0], key_row_table[0], value_row_table[0]
    cols = vertical_cols[0]
    count = n - 2
    per_rank = rows // TILE_COLUMNS
    vmem = pl.BlockSpec(memory_space=pltpu.VMEM)
    smem = pl.BlockSpec(memory_space=pltpu.SMEM)
    params = pltpu.CompilerParams(vmem_limit_bytes=VMEM_BYTES)
    unit = jax.ShapeDtypeStruct((2, rows, kv * HEAD_SIZE), jnp.bfloat16)
    rank1 = rank[None]

    prepared = pl.pallas_call(
        functools.partial(prep_kernel, n, rows, kv),
        out_shape=[unit] * (2 + count)
        + [
            jax.ShapeDtypeStruct((kv, 2, 2 * rows), jnp.float32),
            jax.ShapeDtypeStruct((kv, 1, 2 * rows), jnp.float32),
            jax.ShapeDtypeStruct((kv, 2, count * rows), jnp.float32),
        ],
        in_specs=[smem, smem, vmem, vmem, vmem],
        out_specs=[vmem] * (5 + count),
        scratch_shapes=[
            pltpu.VMEM((2, rows, kv * HEAD_SIZE), jnp.bfloat16),
            pltpu.VMEM((kv, 2 * n * per_rank, TILE_COLUMNS), jnp.float32),
            pltpu.SMEM((kv, n * MAXT), jnp.int32),
            pltpu.SMEM((kv, n), jnp.int32),
        ],
        compiler_params=params,
        name="prep",
    )(rank1, cols, cols, k, v)
    pack0, pack1 = prepared[:2]
    payloads = prepared[2 : 2 + count]
    band_bias, extra_bias, remote_bias = prepared[2 + count :]

    def shifted(x, d):
        return lax.ppermute(x, "ctx", [(i, (i + d) % n) for i in range(n)])

    in0 = shifted(pack0, 1)
    in1 = lax.ppermute(pack1, "ctx", [(i, i + 1) for i in range(n - 1)])
    arrived = [shifted(x, i + 2) for i, x in enumerate(payloads)]

    reach = rows - 1 - jnp.arange(2 * rows, dtype=jnp.int32)
    hit = jnp.any(slash_offsets[0][:, :, None] == reach[None, None, :], axis=1)
    slash = jnp.where(hit, 0.0, DEAD).astype(jnp.float32)[:, None, :]

    state = jax.ShapeDtypeStruct((2, rows, heads * HEAD_SIZE), jnp.float32)
    acc, stat = pl.pallas_call(
        functools.partial(near_kernel, rows, kv, group_size),
        out_shape=[state, state],
        in_specs=[smem] + [vmem] * 8,
        out_specs=[vmem] * 2,
        scratch_shapes=[
            pltpu.VMEM((kv, 2, 2 * rows, HEAD_SIZE), jnp.bfloat16),
            pltpu.VMEM((kv, 2, 2 * rows, 2 * HEAD_SIZE), jnp.bfloat16),
            pltpu.VMEM((kv, 2 * rows, HEAD_SIZE), jnp.bfloat16),
            pltpu.VMEM((kv, 2 * rows, 2 * HEAD_SIZE), jnp.bfloat16),
            pltpu.VMEM((kv, 2, 2, rows // 2, rows // 2), jnp.float32),
        ],
        compiler_params=params,
        cost_estimate=pl.CostEstimate(
            flops=heads * 2 * rows * 6 * rows * HEAD_SIZE * 4, bytes_accessed=16_000_000,
            transcendentals=heads * 6 * rows * rows,
        ),
        name="near",
    )(rank1, q, k, v, in0, in1, band_bias, extra_bias, slash)

    out = pl.pallas_call(
        functools.partial(far_kernel, rows, kv, group_size, count),
        out_shape=jax.ShapeDtypeStruct(q.shape, jnp.bfloat16),
        in_specs=[vmem] * (4 + count),
        out_specs=vmem,
        scratch_shapes=[
            pltpu.VMEM((kv, count * rows, HEAD_SIZE), jnp.bfloat16),
            pltpu.VMEM((kv, count * rows, 2 * HEAD_SIZE), jnp.bfloat16),
        ],
        compiler_params=params,
        cost_estimate=pl.CostEstimate(
            flops=heads * 2 * rows * 2 * count * rows * HEAD_SIZE * 4, bytes_accessed=12_000_000,
            transcendentals=heads * 2 * count * rows * rows,
        ),
        name="far",
    )(q, acc, stat, remote_bias, *arrived)
    return out[None]


def solution(mesh):
    in_specs = (
        P("section", None, ("groups", "ctx"), "head"),
        P("section", None, ("groups", "ctx"), "head"),
        P("section", None, ("groups", "ctx"), "head"),
        P("section", "head", "groups"),
        P("section", "head", "groups"),
    )
    out_specs = P("section", None, ("groups", "ctx"), "head")
    return jax.shard_map(
        per_device, mesh=mesh, in_specs=in_specs, out_specs=out_specs, check_vma=False
    )
```

time: 182 us -> 76.5 us (0.42)
  the two profiles are of different devices: /device:TPU:0 before, /device:TPU:18 now
where the time goes in v1:
time: 76.5 us; the launch traced here: 76.1 us
  Pallas kernels  41.9 us (55%)
  waiting for transfers between devices  19.2 us (25%)
  local copies, waits for them, and re-layouts  8.75 us (11%)
  starting transfers between devices  5.68 us (7%)
    pallas_call x1, Pallas kernels, per_device(): pl.pallas_call(functools.partial(far_kernel, rows, kv, group_size, count)...  21.2 us
    pallas_call x1, Pallas kernels, per_device(): pl.pallas_call(functools.partial(near_kernel, rows, kv, group_size), out_...  19.2 us
    ppermute x1, waiting for transfers between devices, per_device(): in1 = lax.ppermute(pack1, 'ctx', [(i, i + 1) for i in range(n - 1)])  16.9 us
    unnamed x17, local copies, waits for them, and re-layouts  8.72 us
    ppermute x3, starting transfers between devices, shifted(): return lax.ppermute(x, 'ctx', [(i, (i + d) % n) for i in range(n)])  3.56 us
    ppermute x3, waiting for transfers between devices, shifted(): return lax.ppermute(x, 'ctx', [(i, (i + d) % n) for i in range(n)])  2.37 us
    ppermute x1, starting transfers between devices, per_device(): in1 = lax.ppermute(pack1, 'ctx', [(i, i + 1) for i in range(n - 1)])  2.12 us
  transfers between devices with their start and end apart: 4, of which 2 were waited for; matrix products, arithmetic and copies ran while one was open for 2% of the time, Pallas kernels for 25%

profile of v1, /device:TPU:18, one launch (start us, length us, event | category | flops | bytes accessed | tf_op | source)
XLA Modules:
  0.0 76.1 jit_solution(1276700771268307232)
XLA Ops:
  0.0 0.0 copy-start
  0.0 0.9 %copy-done = bf16[1,2,256,256]{3,2,1,0:T(8,128)(2,1)S(1)} copy-done((bf16[1,2,256,256]{3,2,1,0:T(8,128)(2,1)S(1)}, bf16[1,2,256,256]{3,2,1,0:T(8,128)(2,1)}, u32[]{:S(2)}) %copy-start) | copy-done | bytes 262168
  1.0 0.0 copy-start.2
  1.0 0.9 %copy-done.2 = bf16[1,2,256,256]{3,2,1,0:T(8,128)(2,1)S(1)} copy-done((bf16[1,2,256,256]{3,2,1,0:T(8,128)(2,1)S(1)}, bf16[1,2,256,256]{3,2,1,0:T(8,128)(2,1)}, u32[]{:S(2)}) %copy-start.2) | copy-done | bytes 262168
  1.9 0.0 copy-start.4
  1.9 0.7 copy-done.4
  2.6 1.5 %prep.1 = (bf16[2,256,256]{2,1,0:T(8,128)(2,1)S(1)}, bf16[2,256,256]{2,1,0:T(8,128)(2,1)S(1)}, bf16[2,256,256]{2,1,0:T(8,128)(2,1)S(1)}, bf16[2,256,256]{2,1,0:T...) custom-call(s32[1]{0:T(128)} %bitcast.1.rank_ref, ...), custom_call_target="tpu_custom_call" | custom-call | tf_op jit(solution)/shard_map/prep/pallas_call | solution.py:261
  4.1 1.6 %collective-permute-start = (bf16[2,256,256]{2,1,0:T(8,128)(2,1)S(1)}, bf16[2,256,256]{2,1,0:T(8,128)(2,1)S(1)}, u32[]{:S(2)}, u32[]{:S(2)}) collective-permute-start(bf16[2,256,256]{2,1,0:T(8,128)(2,1)S(1)} %get-tuple-element.14), channel_id=1, source_target_pairs={{0,4},{4,8},{8,12},{12,0},{1,5},{5,9},{9,13},{13,1},{2,6},{6,10},{... | collective-permute-start | bytes 786440 | tf_op jit(solution)/shard_map/ppermute | solution.py:285
  5.8 2.1 %collective-permute-start.1 = (bf16[2,256,256]{2,1,0:T(8,128)(2,1)S(1)}, bf16[2,256,256]{2,1,0:T(8,128)(2,1)S(1)}, u32[]{:S(2)}, u32[]{:S(2)}) collective-permute-start(bf16[2,256,256]{2,1,0:T(8,128)(2,1)S(1)} %get-tuple-element.15), channel_id=1, source_target_pairs={{0,4},{4,8},{8,12},{1,5},{5,9},{9,13},{2,6},{6,10},{10,14},{3,7},{... | collective-permute-start | bytes 786440 | tf_op jit(solution)/shard_map/ppermute | solution.py:288
  7.9 1.8 %collective-permute-start.2 = (bf16[2,256,256]{2,1,0:T(8,128)(2,1)S(1)}, bf16[2,256,256]{2,1,0:T(8,128)(2,1)S(1)}, u32[]{:S(2)}, u32[]{:S(2)}) collective-permute-start(bf16[2,256,256]{2,1,0:T(8,128)(2,1)S(1)} %get-tuple-element.21), channel_id=1, source_target_pairs={{0,8},{4,12},{8,0},{12,4},{1,9},{5,13},{9,1},{13,5},{2,10},{6,14},... | collective-permute-start | bytes 786440 | tf_op jit(solution)/shard_map/ppermute | solution.py:285
  9.7 0.2 collective-permute-start.3
  9.8 0.7 copy.8
  10.5 0.4 compare_reduce_fusion
  11.0 2.4 %collective-permute-done.in0_ref = bf16[2,256,256]{2,1,0:T(8,128)(2,1)S(1)} collective-permute-done((bf16[2,256,256]{2,1,0:T(8,128)(2,1)S(1)}, bf16[2,256,256]{2,1,0:T(8,128)(2,1)S(1)}, u32[]{:S(2)}, u32[]{:S(2)}) %collective-permute-start) | collective-permute-done | bytes 262176 | tf_op jit(solution)/shard_map/ppermute | solution.py:285
  13.4 16.9 %collective-permute-done.1.in1_ref = bf16[2,256,256]{2,1,0:T(8,128)(2,1)S(1)} collective-permute-done((bf16[2,256,256]{2,1,0:T(8,128)(2,1)S(1)}, bf16[2,256,256]{2,1,0:T(8,128)(2,1)S(1)}, u32[]{:S(2)}, u32[]{:S(2)}) %collective-permute-start.1) | collective-permute-done | bytes 262176 | tf_op jit(solution)/shard_map/ppermute | solution.py:288
  30.2 0.0 copy-start.1
  30.2 0.9 %copy-done.1 = bf16[1,2,256,256]{3,2,1,0:T(8,128)(2,1)S(1)} copy-done((bf16[1,2,256,256]{3,2,1,0:T(8,128)(2,1)S(1)}, bf16[1,2,256,256]{3,2,1,0:T(8,128)(2,1)}, u32[]{:S(2)}) %copy-start.1) | copy-done | bytes 262168
  31.2 0.0 copy-start.3
  31.2 0.9 %copy-done.3 = bf16[1,2,256,256]{3,2,1,0:T(8,128)(2,1)S(1)} copy-done((bf16[1,2,256,256]{3,2,1,0:T(8,128)(2,1)S(1)}, bf16[1,2,256,256]{3,2,1,0:T(8,128)(2,1)}, u32[]{:S(2)}) %copy-start.3) | copy-done | bytes 262168
  32.1 0.0 copy-start.5
  32.1 1.5 %copy-done.5 = bf16[1,2,256,1792]{3,2,1,0:T(8,128)(2,1)S(1)} copy-done((bf16[1,2,256,1792]{3,2,1,0:T(8,128)(2,1)S(1)}, bf16[1,2,256,1792]{3,2,1,0:T(8,128)(2,1)}, u32[]{:S(2)}) %copy-start.5) | copy-done | bytes 1835032
  33.6 0.0 copy-start.6
  33.6 19.2 %near.1 = (f32[2,256,1792]{2,1,0:T(8,128)}, f32[2,256,1792]{2,1,0:T(8,128)}) custom-call(s32[1]{0:T(128)} %bitcast.1.rank_ref, bf16[2,256,1792]{2,1,0:T(8,128)(2,1)S(1)} %bitcast.15, bf16[2,256,256]{2,1,0:T(8,128)(2,1)S(1)} %bitcast.10, bf16[2,256,256]{2,1,0:T(8,128)(2,1)S(1)} %bitcast.12, bf16[2,256,256]{2,1,0:T(8,128)(2,1)S(1)} %collective-permute-done.in0_ref, ...), custom_call_target="tpu_custom_call" | custom-call | flops 5637144576 | bytes 16000000 | tf_op jit(solution)/shard_map/near/pallas_call | solution.py:296
  52.8 0.0 collective-permute-done.2.refs_4_
  52.8 0.0 collective-permute-done.3.refs_5_
  52.8 0.0 copy-done.6
  52.9 0.0 copy-start.7
  52.9 2.0 %copy-done.7 = f32[2,256,1792]{2,1,0:T(8,128)S(1)} copy-done((f32[2,256,1792]{2,1,0:T(8,128)S(1)}, f32[2,256,1792]{2,1,0:T(8,128)}, u32[]{:S(2)}) %copy-start.7) | copy-done | bytes 3670040
  54.9 21.2 %far.1 = bf16[2,256,1792]{2,1,0:T(8,128)(2,1)} custom-call(bf16[2,256,1792]{2,1,0:T(8,128)(2,1)S(1)} %bitcast.16, f32[2,256,1792]{2,1,0:T(8,128)S(1)} %copy-done.7, f32[2,256,1792]{2,1,0:T(8,128)} %get-tuple-element.19.refs_2_, f32[2,2,512]{2,1,0:T(2,128)S(1)} %get-tuple-element.20.refs_3_, bf16[2,256,256]{2,1,0:T(8,128)(2,1)S(1)} %collective-permute-done.2.refs_4_, ...), custom_call_target="tpu_custom_call" | custom-call | flops 3758096384 | bytes 12000000 | tf_op jit(solution)/shard_map/far/pallas_call | solution.py:316
  (3 shorter events, 0.0 us)
Async XLA Ops:
  0.0 0.9 %copy-start = (bf16[1,2,256,256]{3,2,1,0:T(8,128)(2,1)S(1)}, bf16[1,2,256,256]{3,2,1,0:T(8,128)(2,1)}, u32[]{:S(2)}) copy-start(bf16[1,2,256,256]{3,2,1,0:T(8,128)(2,1)} %param.6) | copy-start | bytes 786436
  1.0 0.9 %copy-start.2 = (bf16[1,2,256,256]{3,2,1,0:T(8,128)(2,1)S(1)}, bf16[1,2,256,256]{3,2,1,0:T(8,128)(2,1)}, u32[]{:S(2)}) copy-start(bf16[1,2,256,256]{3,2,1,0:T(8,128)(2,1)} %param.7) | copy-start | bytes 786436
  1.9 0.7 copy-start.4
  4.1 9.2 %collective-permute-start = (bf16[2,256,256]{2,1,0:T(8,128)(2,1)S(1)}, bf16[2,256,256]{2,1,0:T(8,128)(2,1)S(1)}, u32[]{:S(2)}, u32[]{:S(2)}) collective-permute-start(bf16[2,256,256]{2,1,0:T(8,128)(2,1)S(1)} %get-tuple-element.14), channel_id=1, source_target_pairs={{0,4},{4,8},{8,12},{12,0},{1,5},{5,9},{9,13},{13,1},{2,6},{6,10},{... | collective-permute-start | bytes 786440 | tf_op jit(solution)/shard_map/ppermute | solution.py:285
  5.8 24.5 %collective-permute-start.1 = (bf16[2,256,256]{2,1,0:T(8,128)(2,1)S(1)}, bf16[2,256,256]{2,1,0:T(8,128)(2,1)S(1)}, u32[]{:S(2)}, u32[]{:S(2)}) collective-permute-start(bf16[2,256,256]{2,1,0:T(8,128)(2,1)S(1)} %get-tuple-element.15), channel_id=1, source_target_pairs={{0,4},{4,8},{8,12},{1,5},{5,9},{9,13},{2,6},{6,10},{10,14},{3,7},{... | collective-permute-start | bytes 786440 | tf_op jit(solution)/shard_map/ppermute | solution.py:288
  7.9 45.0 %collective-permute-start.2 = (bf16[2,256,256]{2,1,0:T(8,128)(2,1)S(1)}, bf16[2,256,256]{2,1,0:T(8,128)(2,1)S(1)}, u32[]{:S(2)}, u32[]{:S(2)}) collective-permute-start(bf16[2,256,256]{2,1,0:T(8,128)(2,1)S(1)} %get-tuple-element.21), channel_id=1, source_target_pairs={{0,8},{4,12},{8,0},{12,4},{1,9},{5,13},{9,1},{13,5},{2,10},{6,14},... | collective-permute-start | bytes 786440 | tf_op jit(solution)/shard_map/ppermute | solution.py:285
  9.7 43.2 %collective-permute-start.3 = (bf16[2,256,256]{2,1,0:T(8,128)(2,1)S(1)}, bf16[2,256,256]{2,1,0:T(8,128)(2,1)S(1)}, u32[]{:S(2)}, u32[]{:S(2)}) collective-permute-start(bf16[2,256,256]{2,1,0:T(8,128)(2,1)S(1)} %get-tuple-element.22), channel_id=1, source_target_pairs={{0,12},{4,0},{8,4},{12,8},{1,13},{5,1},{9,5},{13,9},{2,14},{6,2},{... | collective-permute-start | bytes 786440 | tf_op jit(solution)/shard_map/ppermute | solution.py:285
  30.2 1.0 %copy-start.1 = (bf16[1,2,256,256]{3,2,1,0:T(8,128)(2,1)S(1)}, bf16[1,2,256,256]{3,2,1,0:T(8,128)(2,1)}, u32[]{:S(2)}) copy-start(bf16[1,2,256,256]{3,2,1,0:T(8,128)(2,1)} %param.6) | copy-start | bytes 786436
  31.2 0.9 %copy-start.3 = (bf16[1,2,256,256]{3,2,1,0:T(8,128)(2,1)S(1)}, bf16[1,2,256,256]{3,2,1,0:T(8,128)(2,1)}, u32[]{:S(2)}) copy-start(bf16[1,2,256,256]{3,2,1,0:T(8,128)(2,1)} %param.7) | copy-start | bytes 786436
  32.1 1.5 %copy-start.5 = (bf16[1,2,256,1792]{3,2,1,0:T(8,128)(2,1)S(1)}, bf16[1,2,256,1792]{3,2,1,0:T(8,128)(2,1)}, u32[]{:S(2)}) copy-start(bf16[1,2,256,1792]{3,2,1,0:T(8,128)(2,1)} %param.5) | copy-start | bytes 5505028
  33.6 19.2 %copy-start.6 = (bf16[1,2,256,1792]{3,2,1,0:T(8,128)(2,1)S(1)}, bf16[1,2,256,1792]{3,2,1,0:T(8,128)(2,1)}, u32[]{:S(2)}) copy-start(bf16[1,2,256,1792]{3,2,1,0:T(8,128)(2,1)} %param.5) | copy-start | bytes 5505028
  52.9 2.0 %copy-start.7 = (f32[2,256,1792]{2,1,0:T(8,128)S(1)}, f32[2,256,1792]{2,1,0:T(8,128)}, u32[]{:S(2)}) copy-start(f32[2,256,1792]{2,1,0:T(8,128)} %get-tuple-element.18.refs_1_) | copy-start | bytes 11010052

commit v2 on v1

v2 whole, which is shorter than its diff:
```python
import functools
import math

import jax
import jax.numpy as jnp
from jax import lax
from jax.experimental import pallas as pl
from jax.experimental.pallas import tpu as pltpu
from jax.sharding import PartitionSpec as P

HEAD_SIZE = 128
TILE_COLUMNS = 128
MAXT = 2
DEAD = -1e30
SCALE2 = math.log2(math.e) / math.sqrt(HEAD_SIZE)
VMEM_BYTES = 24 * 1024 * 1024
REACH = 100.0


def dot_nt(a, b):
    return lax.dot_general(a, b, (((1,), (1,)), ((), ())), preferred_element_type=jnp.float32)


def dot_nn(a, b):
    return lax.dot_general(a, b, (((1,), (0,)), ((), ())), preferred_element_type=jnp.float32)


def prep_kernel(n, rows, kv, rank_ref, cols_smem, cols_ref, k_ref, v_ref, *outs):
    payload_refs = outs[: n - 2]
    band_bias_ref, extra_bias_ref, remote_bias_ref = outs[n - 2 : n + 1]
    outbox_ref, marks_ref, slot_ref, count_ref = outs[n + 1 :]
    rank = rank_ref[0]
    half_len = rows * n
    tiles = cols_ref.shape[1] // TILE_COLUMNS
    per_rank = rows // TILE_COLUMNS

    for g in range(kv):
        for s in range(n):
            count_ref[g, s] = 0
            for slot in range(MAXT):
                slot_ref[g, s * MAXT + slot] = -1
        for t in range(tiles):
            owner = cols_smem[g, t * TILE_COLUMNS] % half_len // rows
            seen = count_ref[g, owner]
            slot_ref[g, owner * MAXT + seen] = t
            count_ref[g, owner] = seen + 1

    for g in range(kv):
        lanes = slice(g * HEAD_SIZE, (g + 1) * HEAD_SIZE)
        for slot in range(MAXT):
            tile = jnp.maximum(slot_ref[g, rank * MAXT + slot], 0)
            start = pl.multiple_of(tile * TILE_COLUMNS, TILE_COLUMNS)
            half = cols_smem[g, start] // half_len
            within = cols_ref[pl.ds(g, 1), pl.ds(start, TILE_COLUMNS)] % rows
            hit = lax.broadcasted_iota(jnp.int32, (rows, TILE_COLUMNS), 0) == within
            pick = jnp.where(hit, 1.0, 0.0).astype(jnp.bfloat16)
            for which, ref in enumerate((k_ref, v_ref)):
                source = ref[pl.ds(half, 1), :, lanes][0]
                got = lax.dot_general(
                    pick, source, (((0,), (0,)), ((), ())), preferred_element_type=jnp.float32
                )
                outbox_ref[which, slot * TILE_COLUMNS : (slot + 1) * TILE_COLUMNS, lanes] = (
                    got.astype(jnp.bfloat16)
                )
    for i, ref in enumerate(payload_refs):
        d = i + 2

        @pl.when(rank + d < n)
        def _():
            ref[...] = outbox_ref[...]

        @pl.when(rank + d >= n)
        def _():
            ref[0] = k_ref[0]
            ref[1] = v_ref[0]

    blocks = 2 * n * per_rank
    dead_row = jnp.full((1, rows), DEAD, jnp.float32)
    for g in range(kv):
        cols = cols_ref[g : g + 1, :]
        high = lax.broadcasted_iota(jnp.int32, (blocks, cols.shape[1]), 0) == cols // TILE_COLUMNS
        low = lax.broadcasted_iota(jnp.int32, (TILE_COLUMNS, cols.shape[1]), 0) == cols % TILE_COLUMNS
        count = dot_nt(
            jnp.where(high, 1.0, 0.0).astype(jnp.bfloat16),
            jnp.where(low, 1.0, 0.0).astype(jnp.bfloat16),
        )
        marks_ref[g] = jnp.where(count > 0.5, 0.0, DEAD)

        def marks_of(half, s):
            first = (half * n + s) * per_rank
            return jnp.concatenate(
                [marks_ref[g, pl.ds(first + i, 1), :] for i in range(per_rank)], axis=1
            )

        first_rank = rank == 0
        before = jnp.where(first_rank, n - 1, rank - 1)
        before_low = marks_of(0, before)
        own_low = marks_of(0, rank)
        own_high = marks_of(1, rank)
        before_high = marks_of(jnp.where(first_rank, 0, 1), before)
        band_bias_ref[g, 0:1, :rows] = jnp.where(first_rank, dead_row, before_low)
        band_bias_ref[g, 0:1, rows:] = own_low
        band_bias_ref[g, 1:2, :rows] = before_high
        band_bias_ref[g, 1:2, rows:] = own_high
        extra_bias_ref[g, 0:1, :rows] = own_low
        extra_bias_ref[g, 0:1, rows:] = jnp.where(first_rank, dead_row, before_low)
        for i in range(n - 2):
            d = i + 2
            earlier = rank >= d
            s = jnp.where(earlier, rank - d, rank - d + n)
            raw = marks_of(0, s)
            for slot in range(MAXT):
                tile = slot_ref[g, s * MAXT + slot]
                half = cols_smem[g, jnp.maximum(tile, 0) * TILE_COLUMNS] // half_len
                live = tile >= 0
                high_value = jnp.where(live, 0.0, DEAD)
                low_value = jnp.where(live & (half == 0) & earlier, 0.0, DEAD)
                span = slice(i * rows + slot * TILE_COLUMNS, i * rows + (slot + 1) * TILE_COLUMNS)
                part = slice(slot * TILE_COLUMNS, (slot + 1) * TILE_COLUMNS)
                remote_bias_ref[g, 0:1, span] = jnp.full((1, TILE_COLUMNS), low_value, jnp.float32)
                remote_bias_ref[g, 1:2, span] = jnp.where(
                    earlier, jnp.full((1, TILE_COLUMNS), high_value, jnp.float32), raw[:, part]
                )


def lane_sums(x):
    ones = jnp.ones((x.shape[1], HEAD_SIZE), jnp.bfloat16)
    return dot_nn(x.astype(jnp.bfloat16), ones)


def folded(x, op):
    while x.shape[0] > 8:
        half = x.shape[0] // 2
        x = op(x[:half], x[half:])
    return x


def norms(x):
    x = x.astype(jnp.float32)
    return lane_sums(x * x)


def in_range(query_norm, key_norm, lowest):
    bound = jnp.sqrt(jnp.max(query_norm)) * jnp.sqrt(jnp.max(key_norm)) * (1.02 * SCALE2)
    return bound - jnp.min(lowest) <= REACH


def lanes_of(head):
    return pl.ds(pl.multiple_of(head * HEAD_SIZE, HEAD_SIZE), HEAD_SIZE)


def split_keys(k_ref, v_ref, kv, rows, keys_ref, values_ref, second=None):
    ones = jnp.ones((2 * rows, HEAD_SIZE), jnp.bfloat16)
    for g in range(kv):
        lanes = slice(g * HEAD_SIZE, (g + 1) * HEAD_SIZE)
        for ref, to in ((k_ref, keys_ref), (v_ref, values_ref)):
            low, high = ref[0, :, lanes], ref[1, :, lanes]
            to[g, :rows, :HEAD_SIZE] = low
            to[g, rows:, :HEAD_SIZE] = high if second is None else jnp.where(second, low, high)
        values_ref[g, :, HEAD_SIZE:] = ones


def slash_blocks(slash_ref, head, t):
    base = jnp.broadcast_to(slash_ref[head], (t, 4 * t))
    rolled = pltpu.roll(base, 1, 1, stride=1, stride_axis=0)
    return rolled[:, :t], rolled[:, t : 2 * t], rolled[:, 2 * t : 3 * t]


def weights_of(blocks, shift):
    return [jnp.exp2(x - shift).astype(jnp.bfloat16) for x in blocks]


def row_max(blocks):
    x = functools.reduce(jnp.maximum, blocks)
    return jnp.broadcast_to(jnp.max(x, axis=1, keepdims=True), x.shape)


def columns_of(s, count):
    return [s[:, b * HEAD_SIZE : (b + 1) * HEAD_SIZE] for b in range(count)]


def own_kernel(
    rows, kv, group_size,
    q_ref, k_ref, v_ref, band_bias_ref, extra_bias_ref, slash_ref,
    acc_ref, sum_ref, shift_ref, gauge_ref, qcopy_ref,
    keys_ref, values_ref, tri_ref,
):
    t = rows // 2
    tri = lax.broadcasted_iota(jnp.int32, (t, t), 0) >= lax.broadcasted_iota(jnp.int32, (t, t), 1)
    split_keys(k_ref, v_ref, kv, rows, keys_ref, values_ref)
    qcopy_ref[...] = q_ref[...]
    for g in range(kv):
        for m in range(2):
            for b in range(2):
                row = band_bias_ref[g, m : m + 1, rows + b * t : rows + (b + 1) * t]
                tri_ref[g, m, b] = jnp.where(tri, row, DEAD)

    gauge_ref[0] = jnp.zeros((8, HEAD_SIZE), jnp.float32)
    gauge_ref[1] = jnp.full((8, HEAD_SIZE), -DEAD, jnp.float32)
    blank = jnp.zeros((t, t), jnp.bfloat16)
    for g in range(kv):

        def one_head(h, carry):
            head = g * group_size + h
            at = lanes_of(head)
            _, t1, t0 = slash_blocks(slash_ref, head, t)
            for m in range(2):
                q = q_ref[m, :, at]
                s = dot_nt(q, keys_ref[g, : (m + 1) * rows]) * SCALE2
                band = s[:, m * rows :]
                row = band_bias_ref[g, m : m + 1, rows : rows + t]
                top = [band[:t, :t] + jnp.maximum(t0, tri_ref[g, m, 0])]
                low = [
                    band[t:, :t] + jnp.maximum(t1, row),
                    band[t:, t:] + jnp.maximum(t0, tri_ref[g, m, 1]),
                ]
                if m == 1:
                    more = columns_of(s[:, :rows] + extra_bias_ref[g, :, :rows], 2)
                    top = [x[:t] for x in more] + top
                    low = [x[t:] for x in more] + low
                top_shift, low_shift = row_max(top), row_max(low)
                p = jnp.concatenate(
                    [
                        jnp.concatenate(weights_of(top, top_shift) + [blank], axis=1),
                        jnp.concatenate(weights_of(low, low_shift), axis=1),
                    ],
                    axis=0,
                )
                o = dot_nn(p, values_ref[g, : (m + 1) * rows])
                shift = jnp.concatenate([top_shift, low_shift], axis=0)
                acc_ref[m, :, at] = o[:, :HEAD_SIZE]
                sum_ref[m, :, at] = o[:, HEAD_SIZE:]
                shift_ref[m, :, at] = shift
                gauge_ref[0] = jnp.maximum(gauge_ref[0], folded(norms(q), jnp.maximum))
                gauge_ref[1] = jnp.minimum(gauge_ref[1], folded(shift, jnp.minimum))
            return carry

        lax.fori_loop(0, group_size, one_head, 0, unroll=True)


def before_kernel(
    rows, kv, group_size,
    rank_ref, q_ref, k_ref, v_ref, band_bias_ref, extra_bias_ref, slash_ref, gauge_ref,
    acc_in, sum_in, shift_in,
    acc_ref, sum_ref, shift_ref,
    keys_ref, values_ref,
):
    first_rank = rank_ref[0] == 0
    shut = jnp.where(first_rank, DEAD, 0.0)
    t = rows // 2
    split_keys(k_ref, v_ref, kv, rows, keys_ref, values_ref, first_rank)
    key_norm = jnp.zeros((8, HEAD_SIZE), jnp.float32)
    for g in range(kv):
        key_norm = jnp.maximum(key_norm, folded(norms(keys_ref[g]), jnp.maximum))
    fast = in_range(gauge_ref[0], key_norm, gauge_ref[1])

    def scores(g, m, head, q):
        t2, t1, _ = slash_blocks(slash_ref, head, t)
        if m == 0:
            t2, t1 = t2 + shut, t1 + shut
        s = dot_nt(q, keys_ref[g, : (m + 1) * rows]) * SCALE2
        band = s[:, m * rows :]
        row = [band_bias_ref[g, m : m + 1, b * t : (b + 1) * t] for b in range(2)]
        blocks = [
            jnp.concatenate(
                [band[:t, :t] + jnp.maximum(t2, row[0]), band[t:, :t] + row[0]], axis=0
            ),
            jnp.concatenate(
                [
                    band[:t, t:] + jnp.maximum(t1, row[1]),
                    band[t:, t:] + jnp.maximum(t2, row[1]),
                ],
                axis=0,
            ),
        ]
        if m == 1:
            blocks = columns_of(s[:, :rows] + extra_bias_ref[g, :, rows:], 2) + blocks
        return blocks

    def merge(g, m, at, blocks, shift, shrink):
        p = jnp.concatenate(weights_of(blocks, shift), axis=1)
        o = dot_nn(p, values_ref[g, : (m + 1) * rows])
        acc, total = acc_in[m, :, at], sum_in[m, :, at]
        if shrink is not None:
            acc, total = acc * shrink, total * shrink
        acc_ref[m, :, at] = acc + o[:, :HEAD_SIZE]
        sum_ref[m, :, at] = total + o[:, HEAD_SIZE:]

    @pl.when(fast)
    def _():
        for g in range(kv):

            def one_head(h, carry):
                head = g * group_size + h
                at = lanes_of(head)
                for m in range(2):
                    shift = shift_in[m, :, at]
                    merge(g, m, at, scores(g, m, head, q_ref[m, :, at]), shift, None)
                    shift_ref[m, :, at] = shift
                return carry

            lax.fori_loop(0, group_size, one_head, 0, unroll=True)

    @pl.when(jnp.logical_not(fast))
    def _():
        for g in range(kv):

            def one_head(h, carry):
                head = g * group_size + h
                at = lanes_of(head)
                for m in range(2):
                    blocks = scores(g, m, head, q_ref[m, :, at])
                    old = shift_in[m, :, at]
                    shift = jnp.maximum(old, row_max(blocks))
                    merge(g, m, at, blocks, shift, jnp.exp2(old - shift))
                    shift_ref[m, :, at] = shift
                return carry

            lax.fori_loop(0, group_size, one_head, 0)


def far_kernel(rows, kv, group_size, count, *refs):
    q_ref, acc_ref, sum_ref, shift_ref, gauge_ref, remote_bias_ref = refs[:6]
    arrived = refs[6 : 6 + count]
    out_ref, kr_ref, vr_ref = refs[6 + count :]
    ones = jnp.ones((rows, HEAD_SIZE), jnp.bfloat16)
    key_norm = jnp.zeros((8, HEAD_SIZE), jnp.float32)
    for g in range(kv):
        lanes = slice(g * HEAD_SIZE, (g + 1) * HEAD_SIZE)
        for i, ref in enumerate(arrived):
            at = slice(i * rows, (i + 1) * rows)
            k = ref[0, :, lanes]
            key_norm = jnp.maximum(key_norm, folded(norms(k), jnp.maximum))
            kr_ref[g, at, :] = k
            vr_ref[g, at, :HEAD_SIZE] = ref[1, :, lanes]
            vr_ref[g, at, HEAD_SIZE:] = ones
    fast = in_range(gauge_ref[0], key_norm, gauge_ref[1])

    def scores(g, m, q):
        s = dot_nt(q, kr_ref[g]) * SCALE2 + remote_bias_ref[g, m : m + 1, :]
        return columns_of(s, count * rows // HEAD_SIZE)

    def finish(g, m, at, blocks, shift, shrink):
        o = dot_nn(jnp.concatenate(weights_of(blocks, shift), axis=1), vr_ref[g])
        acc, total = acc_ref[m, :, at], sum_ref[m, :, at]
        if shrink is not None:
            acc, total = acc * shrink, total * shrink
        out = (acc + o[:, :HEAD_SIZE]) / (total + o[:, HEAD_SIZE:])
        out_ref[m, :, at] = out.astype(jnp.bfloat16)

    @pl.when(fast)
    def _():
        for g in range(kv):

            def one_head(h, carry):
                at = lanes_of(g * group_size + h)
                for m in range(2):
                    finish(g, m, at, scores(g, m, q_ref[m, :, at]), shift_ref[m, :, at], None)
                return carry

            lax.fori_loop(0, group_size, one_head, 0, unroll=True)

    @pl.when(jnp.logical_not(fast))
    def _():
        for g in range(kv):

            def one_head(h, carry):
                at = lanes_of(g * group_size + h)
                for m in range(2):
                    blocks = scores(g, m, q_ref[m, :, at])
                    old = shift_ref[m, :, at]
                    shift = jnp.maximum(old, row_max(blocks))
                    finish(g, m, at, blocks, shift, jnp.exp2(old - shift))
                return carry

            lax.fori_loop(0, group_size, one_head, 0)


def per_device(queries, key_row_table, value_row_table, vertical_cols, slash_offsets):
    n = lax.axis_size("ctx")
    rank = lax.axis_index("ctx").astype(jnp.int32)
    rows = queries.shape[2]
    kv = key_row_table.shape[3] // HEAD_SIZE
    heads = queries.shape[3] // HEAD_SIZE
    group_size = heads // kv
    q, k, v = queries[0], key_row_table[0], value_row_table[0]
    cols = vertical_cols[0]
    count = n - 2
    per_rank = rows // TILE_COLUMNS
    vmem = pl.BlockSpec(memory_space=pltpu.VMEM)
    smem = pl.BlockSpec(memory_space=pltpu.SMEM)
    params = pltpu.CompilerParams(vmem_limit_bytes=VMEM_BYTES)
    unit = jax.ShapeDtypeStruct((2, rows, kv * HEAD_SIZE), jnp.bfloat16)
    rank1 = rank[None]

    def shifted(x, d):
        return lax.ppermute(x, "ctx", [(i, (i + d) % n) for i in range(n)])

    k_before, v_before = shifted(k, 1), shifted(v, 1)

    prepared = pl.pallas_call(
        functools.partial(prep_kernel, n, rows, kv),
        out_shape=[unit] * count
        + [
            jax.ShapeDtypeStruct((kv, 2, 2 * rows), jnp.float32),
            jax.ShapeDtypeStruct((kv, 1, 2 * rows), jnp.float32),
            jax.ShapeDtypeStruct((kv, 2, count * rows), jnp.float32),
        ],
        in_specs=[smem, smem, vmem, vmem, vmem],
        out_specs=[vmem] * (3 + count),
        scratch_shapes=[
            pltpu.VMEM((2, rows, kv * HEAD_SIZE), jnp.bfloat16),
            pltpu.VMEM((kv, 2 * n * per_rank, TILE_COLUMNS), jnp.float32),
            pltpu.SMEM((kv, n * MAXT), jnp.int32),
            pltpu.SMEM((kv, n), jnp.int32),
        ],
        compiler_params=params,
        name="prep",
    )(rank1, cols, cols, k, v)
    band_bias, extra_bias, remote_bias = prepared[count:]
    arrived = [shifted(x, i + 2) for i, x in enumerate(prepared[:count])]

    reach = rows - 1 - jnp.arange(2 * rows, dtype=jnp.int32)
    hit = jnp.any(slash_offsets[0][:, :, None] == reach[None, None, :], axis=1)
    slash = jnp.where(hit, 0.0, DEAD).astype(jnp.float32)[:, None, :]

    state = jax.ShapeDtypeStruct((2, rows, heads * HEAD_SIZE), jnp.float32)
    keys_scratch = pltpu.VMEM((kv, 2 * rows, HEAD_SIZE), jnp.bfloat16)
    values_scratch = pltpu.VMEM((kv, 2 * rows, 2 * HEAD_SIZE), jnp.bfloat16)

    def cost(blocks):
        return pl.CostEstimate(
            flops=heads * blocks * rows * rows * HEAD_SIZE * 4,
            bytes_accessed=16_000_000,
            transcendentals=heads * blocks * rows * rows,
        )

    acc, total, shift, gauge, qv = pl.pallas_call(
        functools.partial(own_kernel, rows, kv, group_size),
        out_shape=[
            state,
            state,
            state,
            jax.ShapeDtypeStruct((2, 8, HEAD_SIZE), jnp.float32),
            jax.ShapeDtypeStruct(q.shape, q.dtype),
        ],
        in_specs=[vmem] * 6,
        out_specs=[vmem] * 5,
        scratch_shapes=[
            keys_scratch,
            values_scratch,
            pltpu.VMEM((kv, 2, 2, rows // 2, rows // 2), jnp.float32),
        ],
        compiler_params=params,
        cost_estimate=cost(3),
        name="own",
    )(q, k, v, band_bias, extra_bias, slash)

    acc, total, shift = pl.pallas_call(
        functools.partial(before_kernel, rows, kv, group_size),
        out_shape=[state] * 3,
        in_specs=[smem] + [vmem] * 10,
        out_specs=[vmem] * 3,
        scratch_shapes=[keys_scratch, values_scratch],
        input_output_aliases={8: 0, 9: 1, 10: 2},
        compiler_params=params,
        cost_estimate=cost(3),
        name="before",
    )(
        rank1, qv, k_before, v_before, band_bias, extra_bias, slash, gauge, acc, total, shift
    )

    out = pl.pallas_call(
        functools.partial(far_kernel, rows, kv, group_size, count),
        out_shape=jax.ShapeDtypeStruct(q.shape, jnp.bfloat16),
        in_specs=[vmem] * (6 + count),
        out_specs=vmem,
        scratch_shapes=[
            pltpu.VMEM((kv, count * rows, HEAD_SIZE), jnp.bfloat16),
            pltpu.VMEM((kv, count * rows, 2 * HEAD_SIZE), jnp.bfloat16),
        ],
        compiler_params=params,
        cost_estimate=cost(2 * count),
        name="far",
    )(qv, acc, total, shift, gauge, remote_bias, *arrived)
    return out[None]


def solution(mesh):
    in_specs = (
        P("section", None, ("groups", "ctx"), "head"),
        P("section", None, ("groups", "ctx"), "head"),
        P("section", None, ("groups", "ctx"), "head"),
        P("section", "head", "groups"),
        P("section", "head", "groups"),
    )
    out_specs = P("section", None, ("groups", "ctx"), "head")
    return jax.shard_map(
        per_device, mesh=mesh, in_specs=in_specs, out_specs=out_specs, check_vma=False
    )
```

time: 76.5 us -> 50.5 us (0.66)
  waiting for transfers between devices: 19.2 us -> 6.04 us
  Pallas kernels: 41.9 us -> 32 us
  local copies, waits for them, and re-layouts: 8.75 us -> 6.71 us
  starting transfers between devices: 5.68 us -> 4.9 us
    ppermute x1 -> x0, waiting for transfers between devices: 16.9 us -> none  [per_device(): in1 = lax.ppermute(pack1, 'ctx', [(i, i + 1) for i in range(n - 1)])]
    pallas_call x1, Pallas kernels: 21.2 us -> 12.1 us  [per_device(): pl.pallas_call(functools.partial(far_kernel, rows, kv, group_size, count)...]
    ppermute x3 -> x4, waiting for transfers between devices: 2.37 us -> 6.04 us  [shifted(): return lax.ppermute(x, 'ctx', [(i, (i + d) % n) for i in range(n)])]
    ppermute x1 -> x0, starting transfers between devices: 2.12 us -> none  [per_device(): in1 = lax.ppermute(pack1, 'ctx', [(i, i + 1) for i in range(n - 1)])]
    unnamed x17 -> x13, local copies, waits for them, and re-layouts: 8.72 us -> 6.68 us
    ppermute x3 -> x4, starting transfers between devices: 3.56 us -> 4.9 us  [shifted(): return lax.ppermute(x, 'ctx', [(i, (i + d) % n) for i in range(n)])]
    pallas_call x1 -> x2, Pallas kernels: 19.2 us -> 18.3 us  [the longest x1 11.7 us: per_device(): pl.pallas_call(functools.partial(before_kernel, rows, kv, group_size), ou...]
  transfers between devices with their start and end apart: 4 -> 4, of which waited for: 2 -> 1; matrix products, arithmetic and copies ran while one was open for 2% -> 2% of each run, Pallas kernels for 25% -> 40%
where the time goes in v2:
time: 50.5 us; the launch traced here: 50.2 us
  Pallas kernels  32 us (63%)
  local copies, waits for them, and re-layouts  6.71 us (13%)
  waiting for transfers between devices  6.04 us (12%)
  starting transfers between devices  4.9 us (10%)
    pallas_call x1, Pallas kernels, per_device(): pl.pallas_call(functools.partial(far_kernel, rows, kv, group_size, count)...  12.1 us
    pallas_call x1, Pallas kernels, per_device(): pl.pallas_call(functools.partial(before_kernel, rows, kv, group_size), ou...  11.7 us
    unnamed x13, local copies, waits for them, and re-layouts  6.68 us
    pallas_call x1, Pallas kernels, per_device(): pl.pallas_call(functools.partial(own_kernel, rows, kv, group_size), out_s...  6.59 us
    ppermute x4, waiting for transfers between devices, shifted(): return lax.ppermute(x, 'ctx', [(i, (i + d) % n) for i in range(n)])  6.04 us
    ppermute x4, starting transfers between devices, shifted(): return lax.ppermute(x, 'ctx', [(i, (i + d) % n) for i in range(n)])  4.9 us
    pallas_call x1, Pallas kernels, per_device(): pl.pallas_call(functools.partial(prep_kernel, n, rows, kv), out_shape=[un...  1.51 us
  transfers between devices with their start and end apart: 4, of which 1 were waited for; matrix products, arithmetic and copies ran while one was open for 2% of the time, Pallas kernels for 40%

profile of v2, /device:TPU:18, one launch (start us, length us, event | category | flops | bytes accessed | tf_op | source)
XLA Modules:
  0.0 50.2 jit_solution(14503888299371805955)
XLA Ops:
  0.0 1.6 %collective-permute-start = (bf16[2,256,256]{2,1,0:T(8,128)(2,1)}, bf16[2,256,256]{2,1,0:T(8,128)(2,1)S(1)}, u32[]{:S(2)}, u32[]{:S(2)}) collective-permute-start(bf16[2,256,256]{2,1,0:T(8,128)(2,1)} %bitcast.9), channel_id=1, source_target_pairs={{0,4},{4,8},{8,12},{12,0},{1,5},{5,9},{9,13},{13,1},{2,6},{6,10},{... | collective-permute-start | bytes 786440 | tf_op jit(solution)/shard_map/ppermute | solution.py:397
  1.6 0.2 collective-permute-start.1
  1.8 0.0 copy-start
  1.8 0.9 %copy-done = bf16[1,2,256,256]{3,2,1,0:T(8,128)(2,1)S(1)} copy-done((bf16[1,2,256,256]{3,2,1,0:T(8,128)(2,1)S(1)}, bf16[1,2,256,256]{3,2,1,0:T(8,128)(2,1)}, u32[]{:S(2)}) %copy-start) | copy-done | bytes 262168
  2.8 0.0 copy-start.2
  2.8 0.9 %copy-done.2 = bf16[1,2,256,256]{3,2,1,0:T(8,128)(2,1)S(1)} copy-done((bf16[1,2,256,256]{3,2,1,0:T(8,128)(2,1)S(1)}, bf16[1,2,256,256]{3,2,1,0:T(8,128)(2,1)}, u32[]{:S(2)}) %copy-start.2) | copy-done | bytes 262168
  3.7 0.0 copy-start.4
  3.7 0.7 %copy-done.4 = s32[1,2,1024]{2,1,0:T(2,128)S(1)} copy-done((s32[1,2,1024]{2,1,0:T(2,128)S(1)}, s32[1,2,1024]{2,1,0:T(2,128)}, u32[]{:S(2)}) %copy-start.4) | copy-done | bytes 8216
  4.4 1.5 %prep.1 = (bf16[2,256,256]{2,1,0:T(8,128)(2,1)S(1)}, bf16[2,256,256]{2,1,0:T(8,128)(2,1)S(1)}, f32[2,2,512]{2,1,0:T(2,128)S(1)}, f32[2,1,512]{2,1,0:T(1,128)S(1)}, f32[2,2,512]{2,1,0:T(2,128)S(1)}) custom-call(s32[1]{0:T(128)} %bitcast.3.rank_ref, s32[2,1024]{1,0:T(2,128)S(1)} %bitcast.15, s32[2,1024]{1,0:T(2,128)S(1)} %bitcast.16, ...), custom_call_target="tpu_custom_call" | custom-call | tf_op jit(solution)/shard_map/prep/pallas_call | solution.py:401
  5.9 1.8 %collective-permute-start.2 = (bf16[2,256,256]{2,1,0:T(8,128)(2,1)S(1)}, bf16[2,256,256]{2,1,0:T(8,128)(2,1)S(1)}, u32[]{:S(2)}, u32[]{:S(2)}) collective-permute-start(bf16[2,256,256]{2,1,0:T(8,128)(2,1)S(1)} %get-tuple-element.29), channel_id=1, source_target_pairs={{0,8},{4,12},{8,0},{12,4},{1,9},{5,13},{9,1},{13,5},{2,10},{6,14},... | collective-permute-start | bytes 786440 | tf_op jit(solution)/shard_map/ppermute | solution.py:397
  7.7 1.3 %collective-permute-start.3 = (bf16[2,256,256]{2,1,0:T(8,128)(2,1)S(1)}, bf16[2,256,256]{2,1,0:T(8,128)(2,1)S(1)}, u32[]{:S(2)}, u32[]{:S(2)}) collective-permute-start(bf16[2,256,256]{2,1,0:T(8,128)(2,1)S(1)} %get-tuple-element.30), channel_id=1, source_target_pairs={{0,12},{4,0},{8,4},{12,8},{1,13},{5,1},{9,5},{13,9},{2,14},{6,2},{... | collective-permute-start | bytes 786440 | tf_op jit(solution)/shard_map/ppermute | solution.py:397
  9.0 0.7 %copy.11 = s32[1,14,64]{2,1,0:T(8,128)S(1)} copy(s32[1,14,64]{2,0,1:T(1,128)} %param.9) | data formatting | bytes 7168
  9.7 0.4 compare_reduce_fusion
  10.2 0.0 copy-start.1
  10.2 0.9 %copy-done.1 = bf16[1,2,256,256]{3,2,1,0:T(8,128)(2,1)S(1)} copy-done((bf16[1,2,256,256]{3,2,1,0:T(8,128)(2,1)S(1)}, bf16[1,2,256,256]{3,2,1,0:T(8,128)(2,1)}, u32[]{:S(2)}) %copy-start.1) | copy-done | bytes 262168
  11.2 0.0 copy-start.3
  11.2 0.9 %copy-done.3 = bf16[1,2,256,256]{3,2,1,0:T(8,128)(2,1)S(1)} copy-done((bf16[1,2,256,256]{3,2,1,0:T(8,128)(2,1)S(1)}, bf16[1,2,256,256]{3,2,1,0:T(8,128)(2,1)}, u32[]{:S(2)}) %copy-start.3) | copy-done | bytes 262168
  12.1 0.0 copy-start.5
  12.1 1.5 %copy-done.5 = bf16[1,2,256,1792]{3,2,1,0:T(8,128)(2,1)S(1)} copy-done((bf16[1,2,256,1792]{3,2,1,0:T(8,128)(2,1)S(1)}, bf16[1,2,256,1792]{3,2,1,0:T(8,128)(2,1)}, u32[]{:S(2)}) %copy-start.5) | copy-done | bytes 1835032
  13.6 6.6 %own.1 = (f32[2,256,1792]{2,1,0:T(8,128)S(1)}, f32[2,256,1792]{2,1,0:T(8,128)S(1)}, f32[2,256,1792]{2,1,0:T(8,128)S(1)}, f32[2,8,128]{2,1,0:T(8,128)S(1)}, bf16[2,256,1792]{2,1,0:T(8,128)(2,1)S(1)}) custom-call(bf16[2,256,1792]{2,1,0:T(8,128)(2,1)S(1)} %bitcast.17, bf16[2,256,256]{2,1,0:T(8,128)(2,1)S(1)} %bitcast.11, bf16[2,256,256]{2,1,0:T(8,128)(2,1)S(1)} %bitcast.14, ...), custom_call_target="tpu_custom_call" | custom-call | flops 1409286144 | bytes 16000000 | tf_op jit(solution)/shard_map/own/pallas_call | solution.py:438
  20.2 0.0 collective-permute-done.k_ref
  20.2 6.0 %collective-permute-done.1.v_ref = bf16[2,256,256]{2,1,0:T(8,128)(2,1)S(1)} collective-permute-done((bf16[2,256,256]{2,1,0:T(8,128)(2,1)}, bf16[2,256,256]{2,1,0:T(8,128)(2,1)S(1)}, u32[]{:S(2)}, u32[]{:S(2)}) %collective-permute-start.1) | collective-permute-done | bytes 262176 | tf_op jit(solution)/shard_map/ppermute | solution.py:397
  26.3 11.7 %before.1 = (f32[2,256,1792]{2,1,0:T(8,128)S(1)}, f32[2,256,1792]{2,1,0:T(8,128)S(1)}, f32[2,256,1792]{2,1,0:T(8,128)S(1)}) custom-call(s32[1]{0:T(128)} %bitcast.3.rank_ref, bf16[2,256,1792]{2,1,0:T(8,128)(2,1)S(1)} %get-tuple-element.20.q_ref.refs_0_, ...), custom_call_target="tpu_custom_call", output_to_operand_aliasing={{0}: (8, {}), {1}: (9, {}), {2}: (10, {})} | custom-call | flops 1409286144 | bytes 16000000 | tf_op jit(solution)/shard_map/before/pallas_call | solution.py:459
  38.0 0.0 collective-permute-done.2.refs_6_
  38.0 0.0 collective-permute-done.3.refs_7_
  38.0 12.1 %far.1 = bf16[2,256,1792]{2,1,0:T(8,128)(2,1)} custom-call(bf16[2,256,1792]{2,1,0:T(8,128)(2,1)S(1)} %get-tuple-element.20.q_ref.refs_0_, f32[2,256,1792]{2,1,0:T(8,128)S(1)} %get-tuple-element.25.refs_1_, f32[2,256,1792]{2,1,0:T(8,128)S(1)} %get-tuple-element.26.refs_2_, f32[2,256,1792]{2,1,0:T(8,128)S(1)} %get-tuple-element.27.refs_3_, ...), custom_call_target="tpu_custom_call" | custom-call | flops 1879048192 | bytes 16000000 | tf_op jit(solution)/shard_map/far/pallas_call | solution.py:473
  (3 shorter events, 0.0 us)
Async XLA Ops:
  0.0 20.2 %collective-permute-start = (bf16[2,256,256]{2,1,0:T(8,128)(2,1)}, bf16[2,256,256]{2,1,0:T(8,128)(2,1)S(1)}, u32[]{:S(2)}, u32[]{:S(2)}) collective-permute-start(bf16[2,256,256]{2,1,0:T(8,128)(2,1)} %bitcast.9), channel_id=1, source_target_pairs={{0,4},{4,8},{8,12},{12,0},{1,5},{5,9},{9,13},{13,1},{2,6},{6,10},{... | collective-permute-start | bytes 786440 | tf_op jit(solution)/shard_map/ppermute | solution.py:397
  1.6 24.7 %collective-permute-start.1 = (bf16[2,256,256]{2,1,0:T(8,128)(2,1)}, bf16[2,256,256]{2,1,0:T(8,128)(2,1)S(1)}, u32[]{:S(2)}, u32[]{:S(2)}) collective-permute-start(bf16[2,256,256]{2,1,0:T(8,128)(2,1)} %bitcast.12), channel_id=1, source_target_pairs={{0,4},{4,8},{8,12},{12,0},{1,5},{5,9},{9,13},{13,1},{2,6},{6,10},{... | collective-permute-start | bytes 786440 | tf_op jit(solution)/shard_map/ppermute | solution.py:397
  1.8 0.9 %copy-start = (bf16[1,2,256,256]{3,2,1,0:T(8,128)(2,1)S(1)}, bf16[1,2,256,256]{3,2,1,0:T(8,128)(2,1)}, u32[]{:S(2)}) copy-start(bf16[1,2,256,256]{3,2,1,0:T(8,128)(2,1)} %param.6) | copy-start | bytes 786436
  2.8 0.9 %copy-start.2 = (bf16[1,2,256,256]{3,2,1,0:T(8,128)(2,1)S(1)}, bf16[1,2,256,256]{3,2,1,0:T(8,128)(2,1)}, u32[]{:S(2)}) copy-start(bf16[1,2,256,256]{3,2,1,0:T(8,128)(2,1)} %param.7) | copy-start | bytes 786436
  3.7 0.7 %copy-start.4 = (s32[1,2,1024]{2,1,0:T(2,128)S(1)}, s32[1,2,1024]{2,1,0:T(2,128)}, u32[]{:S(2)}) copy-start(s32[1,2,1024]{2,1,0:T(2,128)} %param.8) | copy-start | bytes 24580
  5.9 32.1 %collective-permute-start.2 = (bf16[2,256,256]{2,1,0:T(8,128)(2,1)S(1)}, bf16[2,256,256]{2,1,0:T(8,128)(2,1)S(1)}, u32[]{:S(2)}, u32[]{:S(2)}) collective-permute-start(bf16[2,256,256]{2,1,0:T(8,128)(2,1)S(1)} %get-tuple-element.29), channel_id=1, source_target_pairs={{0,8},{4,12},{8,0},{12,4},{1,9},{5,13},{9,1},{13,5},{2,10},{6,14},... | collective-permute-start | bytes 786440 | tf_op jit(solution)/shard_map/ppermute | solution.py:397
  7.7 30.3 %collective-permute-start.3 = (bf16[2,256,256]{2,1,0:T(8,128)(2,1)S(1)}, bf16[2,256,256]{2,1,0:T(8,128)(2,1)S(1)}, u32[]{:S(2)}, u32[]{:S(2)}) collective-permute-start(bf16[2,256,256]{2,1,0:T(8,128)(2,1)S(1)} %get-tuple-element.30), channel_id=1, source_target_pairs={{0,12},{4,0},{8,4},{12,8},{1,13},{5,1},{9,5},{13,9},{2,14},{6,2},{... | collective-permute-start | bytes 786440 | tf_op jit(solution)/shard_map/ppermute | solution.py:397
  10.2 1.0 %copy-start.1 = (bf16[1,2,256,256]{3,2,1,0:T(8,128)(2,1)S(1)}, bf16[1,2,256,256]{3,2,1,0:T(8,128)(2,1)}, u32[]{:S(2)}) copy-start(bf16[1,2,256,256]{3,2,1,0:T(8,128)(2,1)} %param.6) | copy-start | bytes 786436
  11.2 0.9 %copy-start.3 = (bf16[1,2,256,256]{3,2,1,0:T(8,128)(2,1)S(1)}, bf16[1,2,256,256]{3,2,1,0:T(8,128)(2,1)}, u32[]{:S(2)}) copy-start(bf16[1,2,256,256]{3,2,1,0:T(8,128)(2,1)} %param.7) | copy-start | bytes 786436
  12.1 1.5 %copy-start.5 = (bf16[1,2,256,1792]{3,2,1,0:T(8,128)(2,1)S(1)}, bf16[1,2,256,1792]{3,2,1,0:T(8,128)(2,1)}, u32[]{:S(2)}) copy-start(bf16[1,2,256,1792]{3,2,1,0:T(8,128)(2,1)} %param.5) | copy-start | bytes 5505028

commit v3 on v2

--- a/solution.py
+++ b/solution.py
@@ -26,9 +26,12 @@
 
 
 def prep_kernel(n, rows, kv, rank_ref, cols_smem, cols_ref, k_ref, v_ref, *outs):
-    payload_refs = outs[: n - 2]
-    band_bias_ref, extra_bias_ref, remote_bias_ref = outs[n - 2 : n + 1]
-    outbox_ref, marks_ref, slot_ref, count_ref = outs[n + 1 :]
+    parts = (n - 3) * kv
+    split_refs, whole_ref = outs[:parts], outs[parts]
+    band_bias_ref, extra_bias_ref, remote_bias_ref, kcopy_ref, vcopy_ref = outs[parts + 1 : parts + 6]
+    outbox_ref, marks_ref, slot_ref, count_ref = outs[parts + 6 :]
+    kcopy_ref[...] = k_ref[...]
+    vcopy_ref[...] = v_ref[...]
     rank = rank_ref[0]
     half_len = rows * n
     tiles = cols_ref.shape[1] // TILE_COLUMNS
@@ -62,17 +65,21 @@
                 outbox_ref[which, slot * TILE_COLUMNS : (slot + 1) * TILE_COLUMNS, lanes] = (
                     got.astype(jnp.bfloat16)
                 )
-    for i, ref in enumerate(payload_refs):
-        d = i + 2
-
-        @pl.when(rank + d < n)
+    for i in range(n - 2):
+        later = rank + i + 2 < n
+        refs = [whole_ref] if i == n - 3 else split_refs[i * kv : (i + 1) * kv]
+        wide = kv * HEAD_SIZE // len(refs)
+
+        @pl.when(later)
         def _():
-            ref[...] = outbox_ref[...]
-
-        @pl.when(rank + d >= n)
+            for j, ref in enumerate(refs):
+                ref[...] = outbox_ref[:, :, j * wide : (j + 1) * wide]
+
+        @pl.when(jnp.logical_not(later))
         def _():
-            ref[0] = k_ref[0]
-            ref[1] = v_ref[0]
+            for j, ref in enumerate(refs):
+                ref[0] = k_ref[0, :, j * wide : (j + 1) * wide]
+                ref[1] = v_ref[0, :, j * wide : (j + 1) * wide]
 
     blocks = 2 * n * per_rank
     dead_row = jnp.full((1, rows), DEAD, jnp.float32)
@@ -149,14 +156,13 @@
     return pl.ds(pl.multiple_of(head * HEAD_SIZE, HEAD_SIZE), HEAD_SIZE)
 
 
-def split_keys(k_ref, v_ref, kv, rows, keys_ref, values_ref, second=None):
+def split_keys(k_ref, v_ref, kv, rows, keys_ref, values_ref):
     ones = jnp.ones((2 * rows, HEAD_SIZE), jnp.bfloat16)
     for g in range(kv):
         lanes = slice(g * HEAD_SIZE, (g + 1) * HEAD_SIZE)
         for ref, to in ((k_ref, keys_ref), (v_ref, values_ref)):
-            low, high = ref[0, :, lanes], ref[1, :, lanes]
-            to[g, :rows, :HEAD_SIZE] = low
-            to[g, rows:, :HEAD_SIZE] = high if second is None else jnp.where(second, low, high)
+            to[g, :rows, :HEAD_SIZE] = ref[0, :, lanes]
+            to[g, rows:, :HEAD_SIZE] = ref[1, :, lanes]
         values_ref[g, :, HEAD_SIZE:] = ones
 
 
@@ -179,16 +185,37 @@
     return [s[:, b * HEAD_SIZE : (b + 1) * HEAD_SIZE] for b in range(count)]
 
 
+def make_slash(offsets_ref, slash_ref, rows, heads):
+    count = offsets_ref.shape[2]
+    reach = rows - 1 - lax.broadcasted_iota(jnp.int32, (rows, count), 0)
+    ones = jnp.ones((8, count), jnp.bfloat16)
+    for head in range(heads):
+        hit = jnp.where(reach == offsets_ref[head], 1.0, 0.0).astype(jnp.bfloat16)
+        found = dot_nt(ones, hit)[:1]
+        slash_ref[head, :, :rows] = jnp.where(found > 0.5, 0.0, DEAD)
+        slash_ref[head, :, rows:] = jnp.full((1, rows), DEAD, jnp.float32)
+
+
+def hold_kernel(rows, heads, late, offsets_ref, q_ref, *refs):
+    slash_ref, qcopy_ref = refs[late : late + 2]
+    make_slash(offsets_ref, slash_ref, rows, heads)
+    qcopy_ref[...] = q_ref[...]
+    for a, b in zip(refs[:late], refs[late + 2 :]):
+        b[...] = a[...]
+
+
 def own_kernel(
     rows, kv, group_size,
-    q_ref, k_ref, v_ref, band_bias_ref, extra_bias_ref, slash_ref,
-    acc_ref, sum_ref, shift_ref, gauge_ref, qcopy_ref,
-    keys_ref, values_ref, tri_ref,
+    q_ref, k_ref, v_ref, band_bias_ref, extra_bias_ref, slash_ref, *refs,
 ):
+    passed = (len(refs) - 8) // 2
+    for a, b in zip(refs[:passed], refs[passed + 5 :]):
+        b[...] = a[...]
+    acc_ref, sum_ref, shift_ref, gauge_ref, table_ref = refs[passed : passed + 5]
+    keys_ref, values_ref, tri_ref = refs[-3:]
     t = rows // 2
     tri = lax.broadcasted_iota(jnp.int32, (t, t), 0) >= lax.broadcasted_iota(jnp.int32, (t, t), 1)
     split_keys(k_ref, v_ref, kv, rows, keys_ref, values_ref)
-    qcopy_ref[...] = q_ref[...]
     for g in range(kv):
         for m in range(2):
             for b in range(2):
@@ -203,7 +230,9 @@
         def one_head(h, carry):
             head = g * group_size + h
             at = lanes_of(head)
-            _, t1, t0 = slash_blocks(slash_ref, head, t)
+            t2, t1, t0 = slash_blocks(slash_ref, head, t)
+            table_ref[head, :, :t] = t2
+            table_ref[head, :, t:] = t1
             for m in range(2):
                 q = q_ref[m, :, at]
                 s = dot_nt(q, keys_ref[g, : (m + 1) * rows]) * SCALE2
@@ -238,28 +267,37 @@
         lax.fori_loop(0, group_size, one_head, 0, unroll=True)
 
 
-def before_kernel(
+def middle_kernel(
     rows, kv, group_size,
-    rank_ref, q_ref, k_ref, v_ref, band_bias_ref, extra_bias_ref, slash_ref, gauge_ref,
-    acc_in, sum_in, shift_in,
+    rank_ref, q_ref, k_ref, v_ref, first_ref, band_bias_ref, extra_bias_ref, remote_bias_ref,
+    table_ref, gauge_ref, acc_in, sum_in, shift_in,
     acc_ref, sum_ref, shift_ref,
     keys_ref, values_ref,
 ):
     first_rank = rank_ref[0] == 0
     shut = jnp.where(first_rank, DEAD, 0.0)
     t = rows // 2
-    split_keys(k_ref, v_ref, kv, rows, keys_ref, values_ref, first_rank)
+    ones = jnp.ones((3 * rows, HEAD_SIZE), jnp.bfloat16)
     key_norm = jnp.zeros((8, HEAD_SIZE), jnp.float32)
     for g in range(kv):
-        key_norm = jnp.maximum(key_norm, folded(norms(keys_ref[g]), jnp.maximum))
+        lanes = slice(g * HEAD_SIZE, (g + 1) * HEAD_SIZE)
+        for which, ref, to in ((0, k_ref, keys_ref), (1, v_ref, values_ref)):
+            low, high = ref[0, :, lanes], ref[1, :, lanes]
+            to[g, :rows, :HEAD_SIZE] = jnp.where(first_rank, low, high)
+            to[g, rows : 2 * rows, :HEAD_SIZE] = low
+            to[g, 2 * rows :, :HEAD_SIZE] = first_ref[which, :, lanes]
+        values_ref[g, :, HEAD_SIZE:] = ones
+        for part in range(3):
+            k = keys_ref[g, part * rows : (part + 1) * rows]
+            key_norm = jnp.maximum(key_norm, folded(norms(k), jnp.maximum))
     fast = in_range(gauge_ref[0], key_norm, gauge_ref[1])
 
     def scores(g, m, head, q):
-        t2, t1, _ = slash_blocks(slash_ref, head, t)
+        t2, t1 = table_ref[head, :, :t], table_ref[head, :, t:]
         if m == 0:
             t2, t1 = t2 + shut, t1 + shut
-        s = dot_nt(q, keys_ref[g, : (m + 1) * rows]) * SCALE2
-        band = s[:, m * rows :]
+        s = dot_nt(q, keys_ref[g, (1 - m) * rows :]) * SCALE2
+        band = s[:, :rows]
         row = [band_bias_ref[g, m : m + 1, b * t : (b + 1) * t] for b in range(2)]
         blocks = [
             jnp.concatenate(
@@ -274,12 +312,12 @@
             ),
         ]
         if m == 1:
-            blocks = columns_of(s[:, :rows] + extra_bias_ref[g, :, rows:], 2) + blocks
-        return blocks
+            blocks += columns_of(s[:, rows : 2 * rows] + extra_bias_ref[g, :, rows:], 2)
+        return blocks + columns_of(s[:, (m + 1) * rows :] + remote_bias_ref[g, m : m + 1, -rows:], 2)
 
     def merge(g, m, at, blocks, shift, shrink):
         p = jnp.concatenate(weights_of(blocks, shift), axis=1)
-        o = dot_nn(p, values_ref[g, : (m + 1) * rows])
+        o = dot_nn(p, values_ref[g, (1 - m) * rows :])
         acc, total = acc_in[m, :, at], sum_in[m, :, at]
         if shrink is not None:
             acc, total = acc * shrink, total * shrink
@@ -319,61 +357,64 @@
             lax.fori_loop(0, group_size, one_head, 0)
 
 
-def far_kernel(rows, kv, group_size, count, *refs):
+def far_kernel(rows, g, group_size, count, *refs):
     q_ref, acc_ref, sum_ref, shift_ref, gauge_ref, remote_bias_ref = refs[:6]
     arrived = refs[6 : 6 + count]
-    out_ref, kr_ref, vr_ref = refs[6 + count :]
+    out_hbm, keys_ref, values_ref, out_ref, sems = refs[-5:]
     ones = jnp.ones((rows, HEAD_SIZE), jnp.bfloat16)
     key_norm = jnp.zeros((8, HEAD_SIZE), jnp.float32)
-    for g in range(kv):
-        lanes = slice(g * HEAD_SIZE, (g + 1) * HEAD_SIZE)
-        for i, ref in enumerate(arrived):
-            at = slice(i * rows, (i + 1) * rows)
-            k = ref[0, :, lanes]
-            key_norm = jnp.maximum(key_norm, folded(norms(k), jnp.maximum))
-            kr_ref[g, at, :] = k
-            vr_ref[g, at, :HEAD_SIZE] = ref[1, :, lanes]
-            vr_ref[g, at, HEAD_SIZE:] = ones
+    for i, ref in enumerate(arrived):
+        at = slice(i * rows, (i + 1) * rows)
+        k = ref[0]
+        key_norm = jnp.maximum(key_norm, folded(norms(k), jnp.maximum))
+        keys_ref[at, :] = k
+        values_ref[at, :HEAD_SIZE] = ref[1]
+        values_ref[at, HEAD_SIZE:] = ones
     fast = in_range(gauge_ref[0], key_norm, gauge_ref[1])
-
-    def scores(g, m, q):
-        s = dot_nt(q, kr_ref[g]) * SCALE2 + remote_bias_ref[g, m : m + 1, :]
+    copies = [
+        pltpu.make_async_copy(
+            out_ref.at[h], out_hbm.at[:, :, lanes_of(g * group_size + h)], sems.at[h]
+        )
+        for h in range(group_size)
+    ]
+
+    def scores(m, q):
+        bias = remote_bias_ref[g, m : m + 1, : count * rows]
+        s = dot_nt(q, keys_ref[...]) * SCALE2 + bias
         return columns_of(s, count * rows // HEAD_SIZE)
 
-    def finish(g, m, at, blocks, shift, shrink):
-        o = dot_nn(jnp.concatenate(weights_of(blocks, shift), axis=1), vr_ref[g])
+    def finish(h, m, at, blocks, shift, shrink):
+        o = dot_nn(jnp.concatenate(weights_of(blocks, shift), axis=1), values_ref[...])
         acc, total = acc_ref[m, :, at], sum_ref[m, :, at]
         if shrink is not None:
             acc, total = acc * shrink, total * shrink
         out = (acc + o[:, :HEAD_SIZE]) / (total + o[:, HEAD_SIZE:])
-        out_ref[m, :, at] = out.astype(jnp.bfloat16)
-
-    @pl.when(fast)
-    def _():
-        for g in range(kv):
-
-            def one_head(h, carry):
-                at = lanes_of(g * group_size + h)
-                for m in range(2):
-                    finish(g, m, at, scores(g, m, q_ref[m, :, at]), shift_ref[m, :, at], None)
-                return carry
-
-            lax.fori_loop(0, group_size, one_head, 0, unroll=True)
+        out_ref[h, m] = out.astype(jnp.bfloat16)
+
+    for h in range(group_size):
+        at = lanes_of(g * group_size + h)
+        for m in range(2):
+            finish(h, m, at, scores(m, q_ref[m, :, at]), shift_ref[m, :, at], None)
+        copies[h].start()
+    for copy in copies:
+        copy.wait()
 
     @pl.when(jnp.logical_not(fast))
     def _():
-        for g in range(kv):
-
-            def one_head(h, carry):
-                at = lanes_of(g * group_size + h)
-                for m in range(2):
-                    blocks = scores(g, m, q_ref[m, :, at])
-                    old = shift_ref[m, :, at]
-                    shift = jnp.maximum(old, row_max(blocks))
-                    finish(g, m, at, blocks, shift, jnp.exp2(old - shift))
-                return carry
-
-            lax.fori_loop(0, group_size, one_head, 0)
+        def one_head(h, carry):
+            at = lanes_of(g * group_size + h)
+            for m in range(2):
+                blocks = scores(m, q_ref[m, :, at])
+                old = shift_ref[m, :, at]
+                shift = jnp.maximum(old, row_max(blocks))
+                finish(h, m, at, blocks, shift, jnp.exp2(old - shift))
+            return carry
+
+        lax.fori_loop(0, group_size, one_head, 0)
+        for copy in copies:
+            copy.start()
+        for copy in copies:
+            copy.wait()
 
 
 def per_device(queries, key_row_table, value_row_table, vertical_cols, slash_offsets):
@@ -385,12 +426,16 @@
     group_size = heads // kv
     q, k, v = queries[0], key_row_table[0], value_row_table[0]
     cols = vertical_cols[0]
+    offsets = jnp.swapaxes(slash_offsets, 0, 1)
     count = n - 2
+    late = n - 3
     per_rank = rows // TILE_COLUMNS
     vmem = pl.BlockSpec(memory_space=pltpu.VMEM)
     smem = pl.BlockSpec(memory_space=pltpu.SMEM)
+    hbm = pl.BlockSpec(memory_space=pl.ANY)
     params = pltpu.CompilerParams(vmem_limit_bytes=VMEM_BYTES)
     unit = jax.ShapeDtypeStruct((2, rows, kv * HEAD_SIZE), jnp.bfloat16)
+    piece = jax.ShapeDtypeStruct((2, rows, HEAD_SIZE), jnp.bfloat16)
     rank1 = rank[None]
 
     def shifted(x, d):
@@ -400,14 +445,17 @@
 
     prepared = pl.pallas_call(
         functools.partial(prep_kernel, n, rows, kv),
-        out_shape=[unit] * count
+        out_shape=[piece] * (late * kv)
+        + [unit]
         + [
             jax.ShapeDtypeStruct((kv, 2, 2 * rows), jnp.float32),
             jax.ShapeDtypeStruct((kv, 1, 2 * rows), jnp.float32),
             jax.ShapeDtypeStruct((kv, 2, count * rows), jnp.float32),
+            jax.ShapeDtypeStruct(k.shape, k.dtype),
+            jax.ShapeDtypeStruct(v.shape, v.dtype),
         ],
         in_specs=[smem, smem, vmem, vmem, vmem],
-        out_specs=[vmem] * (3 + count),
+        out_specs=[vmem] * (6 + late * kv),
         scratch_shapes=[
             pltpu.VMEM((2, rows, kv * HEAD_SIZE), jnp.bfloat16),
             pltpu.VMEM((kv, 2 * n * per_rank, TILE_COLUMNS), jnp.float32),
@@ -417,12 +465,9 @@
         compiler_params=params,
         name="prep",
     )(rank1, cols, cols, k, v)
-    band_bias, extra_bias, remote_bias = prepared[count:]
-    arrived = [shifted(x, i + 2) for i, x in enumerate(prepared[:count])]
-
-    reach = rows - 1 - jnp.arange(2 * rows, dtype=jnp.int32)
-    hit = jnp.any(slash_offsets[0][:, :, None] == reach[None, None, :], axis=1)
-    slash = jnp.where(hit, 0.0, DEAD).astype(jnp.float32)[:, None, :]
+    pieces = prepared[: late * kv]
+    whole, band_bias, extra_bias, remote_bias, kv_k, kv_v = prepared[late * kv :]
+    first = shifted(whole, n - 1)
 
     state = jax.ShapeDtypeStruct((2, rows, heads * HEAD_SIZE), jnp.float32)
     keys_scratch = pltpu.VMEM((kv, 2 * rows, HEAD_SIZE), jnp.bfloat16)
@@ -435,17 +480,33 @@
             transcendentals=heads * blocks * rows * rows,
         )
 
-    acc, total, shift, gauge, qv = pl.pallas_call(
+    slash, qv, *held = pl.pallas_call(
+        functools.partial(hold_kernel, rows, heads, late),
+        out_shape=[
+            jax.ShapeDtypeStruct((heads, 1, 2 * rows), jnp.float32),
+            jax.ShapeDtypeStruct(q.shape, q.dtype),
+        ]
+        + [piece] * late,
+        in_specs=[vmem] * (2 + late),
+        out_specs=[vmem] * (2 + late),
+        compiler_params=params,
+        name="hold",
+    )(offsets, q, *pieces[::kv])
+    arrived = [[shifted(x, i + 2) for i, x in enumerate(held)]]
+
+    rest = [x for i, x in enumerate(pieces) if i % kv]
+    acc, total, shift, gauge, table, *rest = pl.pallas_call(
         functools.partial(own_kernel, rows, kv, group_size),
         out_shape=[
             state,
             state,
             state,
             jax.ShapeDtypeStruct((2, 8, HEAD_SIZE), jnp.float32),
-            jax.ShapeDtypeStruct(q.shape, q.dtype),
-        ],
-        in_specs=[vmem] * 6,
-        out_specs=[vmem] * 5,
+            jax.ShapeDtypeStruct((heads, rows // 2, rows), jnp.float32),
+        ]
+        + [piece] * len(rest),
+        in_specs=[vmem] * (6 + len(rest)),
+        out_specs=[vmem] * (5 + len(rest)),
         scratch_shapes=[
             keys_scratch,
             values_scratch,
@@ -454,36 +515,49 @@
         compiler_params=params,
         cost_estimate=cost(3),
         name="own",
-    )(q, k, v, band_bias, extra_bias, slash)
+    )(qv, kv_k, kv_v, band_bias, extra_bias, slash, *rest)
+    for g in range(kv - 1):
+        arrived.append([shifted(x, i + 2) for i, x in enumerate(rest[g :: kv - 1])])
 
     acc, total, shift = pl.pallas_call(
-        functools.partial(before_kernel, rows, kv, group_size),
+        functools.partial(middle_kernel, rows, kv, group_size),
         out_shape=[state] * 3,
-        in_specs=[smem] + [vmem] * 10,
+        in_specs=[smem] + [vmem] * 12,
         out_specs=[vmem] * 3,
-        scratch_shapes=[keys_scratch, values_scratch],
-        input_output_aliases={8: 0, 9: 1, 10: 2},
+        scratch_shapes=[
+            pltpu.VMEM((kv, 3 * rows, HEAD_SIZE), jnp.bfloat16),
+            pltpu.VMEM((kv, 3 * rows, 2 * HEAD_SIZE), jnp.bfloat16),
+        ],
+        input_output_aliases={10: 0, 11: 1, 12: 2},
         compiler_params=params,
-        cost_estimate=cost(3),
-        name="before",
+        cost_estimate=cost(5),
+        name="middle",
     )(
-        rank1, qv, k_before, v_before, band_bias, extra_bias, slash, gauge, acc, total, shift
+        rank1, qv, k_before, v_before, first, band_bias, extra_bias, remote_bias, table, gauge,
+        acc, total, shift,
     )
 
-    out = pl.pallas_call(
-        functools.partial(far_kernel, rows, kv, group_size, count),
-        out_shape=jax.ShapeDtypeStruct(q.shape, jnp.bfloat16),
-        in_specs=[vmem] * (6 + count),
-        out_specs=vmem,
-        scratch_shapes=[
-            pltpu.VMEM((kv, count * rows, HEAD_SIZE), jnp.bfloat16),
-            pltpu.VMEM((kv, count * rows, 2 * HEAD_SIZE), jnp.bfloat16),
-        ],
-        compiler_params=params,
-        cost_estimate=cost(2 * count),
-        name="far",
-    )(qv, acc, total, shift, gauge, remote_bias, *arrived)
-    return out[None]
+    out = []
+    for g in range(kv):
+        out = [
+            pl.pallas_call(
+                functools.partial(far_kernel, rows, g, group_size, late),
+                out_shape=jax.ShapeDtypeStruct(q.shape, jnp.bfloat16),
+                in_specs=[vmem] * (6 + late) + [hbm] * len(out),
+                out_specs=hbm,
+                scratch_shapes=[
+                    pltpu.VMEM((late * rows, HEAD_SIZE), jnp.bfloat16),
+                    pltpu.VMEM((late * rows, 2 * HEAD_SIZE), jnp.bfloat16),
+                    pltpu.VMEM((group_size, 2, rows, HEAD_SIZE), jnp.bfloat16),
+                    pltpu.SemaphoreType.DMA((group_size,)),
+                ],
+                input_output_aliases={6 + late: 0} if out else {},
+                compiler_params=params,
+                cost_estimate=cost(late),
+                name="far",
+            )(qv, acc, total, shift, gauge, remote_bias, *arrived[g], *out)
+        ]
+    return out[0][None]
 
 
 def solution(mesh):

time: 50.5 us -> 54.4 us (1.077)
  Pallas kernels: 32 us -> 36.2 us
  local copies, waits for them, and re-layouts: 6.71 us -> 4.79 us
  starting transfers between devices: 4.9 us -> 6.71 us
    pallas_call x3 -> x5, Pallas kernels: 25.4 us -> 29.6 us  [the longest x1 14.6 us: per_device(): pl.pallas_call(functools.partial(middle_kernel, rows, kv, group_size), ou...]
    unnamed x13 -> x10, local copies, waits for them, and re-layouts: 6.68 us -> 4.79 us
    ppermute x4 -> x5, starting transfers between devices: 4.9 us -> 6.71 us  [shifted(): return lax.ppermute(x, 'ctx', [(i, (i + d) % n) for i in range(n)])]
    ppermute x4 -> x5, waiting for transfers between devices: 6.04 us -> 6.21 us  [shifted(): return lax.ppermute(x, 'ctx', [(i, (i + d) % n) for i in range(n)])]
  transfers between devices with their start and end apart: 4 -> 5, of which waited for: 1 -> 1; matrix products, arithmetic and copies ran while one was open for 2% -> 0% of each run, Pallas kernels for 40% -> 55%
where the time goes in v3:
time: 54.4 us; the launch traced here: 54.1 us
  Pallas kernels  36.2 us (67%)
  starting transfers between devices  6.71 us (12%)
  waiting for transfers between devices  6.21 us (11%)
  local copies, waits for them, and re-layouts  4.79 us (9%)
    pallas_call x1, Pallas kernels, per_device(): pl.pallas_call(functools.partial(middle_kernel, rows, kv, group_size), ou...  14.6 us
    pallas_call x2, Pallas kernels, per_device(): pl.pallas_call(functools.partial(far_kernel, rows, g, group_size, late),...  13 us
    ppermute x5, starting transfers between devices, shifted(): return lax.ppermute(x, 'ctx', [(i, (i + d) % n) for i in range(n)])  6.71 us
    pallas_call x1, Pallas kernels, per_device(): pl.pallas_call(functools.partial(own_kernel, rows, kv, group_size), out_s...  6.62 us
    ppermute x5, waiting for transfers between devices, shifted(): return lax.ppermute(x, 'ctx', [(i, (i + d) % n) for i in range(n)])  6.21 us
    unnamed x10, local copies, waits for them, and re-layouts  4.79 us
    pallas_call x1, Pallas kernels, per_device(): pl.pallas_call(functools.partial(prep_kernel, n, rows, kv), out_shape=[pi...  1.55 us
  transfers between devices with their start and end apart: 5, of which 1 were waited for; matrix products, arithmetic and copies ran while one was open for 0% of the time, Pallas kernels for 55%

profile of v3, /device:TPU:18, one launch (start us, length us, event | category | flops | bytes accessed | tf_op | source)
XLA Modules:
  0.0 54.1 jit_solution(7720345537820677386)
XLA Ops:
  0.0 1.6 %collective-permute-start = (bf16[2,256,256]{2,1,0:T(8,128)(2,1)}, bf16[2,256,256]{2,1,0:T(8,128)(2,1)S(1)}, u32[]{:S(2)}, u32[]{:S(2)}) collective-permute-start(bf16[2,256,256]{2,1,0:T(8,128)(2,1)} %bitcast.8), channel_id=1, source_target_pairs={{0,4},{4,8},{8,12},{12,0},{1,5},{5,9},{9,13},{13,1},{2,6},{6,10},{... | collective-permute-start | bytes 786440 | tf_op jit(solution)/shard_map/ppermute | solution.py:442
  1.6 0.2 collective-permute-start.1
  1.8 0.0 copy-start.1
  1.8 0.9 %copy-done.1 = bf16[1,2,256,256]{3,2,1,0:T(8,128)(2,1)S(1)} copy-done((bf16[1,2,256,256]{3,2,1,0:T(8,128)(2,1)S(1)}, bf16[1,2,256,256]{3,2,1,0:T(8,128)(2,1)}, u32[]{:S(2)}) %copy-start.1) | copy-done | bytes 262168
  2.8 0.0 copy-start.2
  2.8 0.9 %copy-done.2 = bf16[1,2,256,256]{3,2,1,0:T(8,128)(2,1)S(1)} copy-done((bf16[1,2,256,256]{3,2,1,0:T(8,128)(2,1)S(1)}, bf16[1,2,256,256]{3,2,1,0:T(8,128)(2,1)}, u32[]{:S(2)}) %copy-start.2) | copy-done | bytes 262168
  3.7 0.0 copy-start.3
  3.7 0.7 %copy-done.3 = s32[1,2,1024]{2,1,0:T(2,128)S(1)} copy-done((s32[1,2,1024]{2,1,0:T(2,128)S(1)}, s32[1,2,1024]{2,1,0:T(2,128)}, u32[]{:S(2)}) %copy-start.3) | copy-done | bytes 8216
  4.4 1.5 %prep.1 = (bf16[2,256,128]{2,1,0:T(8,128)(2,1)S(1)}, bf16[2,256,128]{2,1,0:T(8,128)(2,1)S(1)}, bf16[2,256,256]{2,1,0:T(8,128)(2,1)S(1)}, f32[2,2,512]{2,1,0:T(2,...) custom-call(s32[1]{0:T(128)} %bitcast.2.rank_ref, ...), custom_call_target="tpu_custom_call" | custom-call | tf_op jit(solution)/shard_map/prep/pallas_call | solution.py:446
  6.0 1.9 %collective-permute-start.2 = (bf16[2,256,256]{2,1,0:T(8,128)(2,1)S(1)}, bf16[2,256,256]{2,1,0:T(8,128)(2,1)S(1)}, u32[]{:S(2)}, u32[]{:S(2)}) collective-permute-start(bf16[2,256,256]{2,1,0:T(8,128)(2,1)S(1)} %get-tuple-element.27), channel_id=1, source_target_pairs={{0,12},{4,0},{8,4},{12,8},{1,13},{5,1},{9,5},{13,9},{2,14},{6,2},{... | collective-permute-start | bytes 786440 | tf_op jit(solution)/shard_map/ppermute | solution.py:442
  7.8 0.0 copy-start
  7.8 1.5 %copy-done = bf16[1,2,256,1792]{3,2,1,0:T(8,128)(2,1)S(1)} copy-done((bf16[1,2,256,1792]{3,2,1,0:T(8,128)(2,1)S(1)}, bf16[1,2,256,1792]{3,2,1,0:T(8,128)(2,1)}, u32[]{:S(2)}) %copy-start) | copy-done | bytes 1835032
  9.3 0.0 copy-start.4
  9.3 0.7 %copy-done.4 = s32[1,14,64]{2,0,1:T(1,128)S(1)} copy-done((s32[1,14,64]{2,0,1:T(1,128)S(1)}, s32[1,14,64]{2,0,1:T(1,128)}, u32[]{:S(2)}) %copy-start.4) | copy-done | bytes 3608
  10.0 0.4 hold.1
  10.4 2.2 %collective-permute-start.4 = (bf16[2,256,128]{2,1,0:T(8,128)(2,1)S(1)}, bf16[2,256,128]{2,1,0:T(8,128)(2,1)S(1)}, u32[]{:S(2)}, u32[]{:S(2)}) collective-permute-start(bf16[2,256,128]{2,1,0:T(8,128)(2,1)S(1)} %get-tuple-element.44), channel_id=1, source_target_pairs={{0,8},{4,12},{8,0},{12,4},{1,9},{5,13},{9,1},{13,5},{2,10},{6,14},... | collective-permute-start | bytes 393224 | tf_op jit(solution)/shard_map/ppermute | solution.py:442
  12.6 6.6 %own.1 = (f32[2,256,1792]{2,1,0:T(8,128)S(1)}, f32[2,256,1792]{2,1,0:T(8,128)S(1)}, f32[2,256,1792]{2,1,0:T(8,128)S(1)}, f32[2,8,128]{2,1,0:T(8,128)S(1)}, f32[1...) custom-call(bf16[2,256,1792]{2,1,0:T(8,128)(2,1)S(1)} %get-tuple-element.26.q_ref.refs_0_, ...), custom_call_target="tpu_custom_call" | custom-call | flops 1409286144 | bytes 16000000 | tf_op jit(solution)/shard_map/own/pallas_call | solution.py:498
  19.2 0.9 %collective-permute-start.3 = (bf16[2,256,128]{2,1,0:T(8,128)(2,1)S(1)}, bf16[2,256,128]{2,1,0:T(8,128)(2,1)S(1)}, u32[]{:S(2)}, u32[]{:S(2)}) collective-permute-start(bf16[2,256,128]{2,1,0:T(8,128)(2,1)S(1)} %get-tuple-element.43), channel_id=1, source_target_pairs={{0,8},{4,12},{8,0},{12,4},{1,9},{5,13},{9,1},{13,5},{2,10},{6,14},... | collective-permute-start | bytes 393224 | tf_op jit(solution)/shard_map/ppermute | solution.py:442
  20.1 0.0 collective-permute-done.k_ref
  20.1 6.2 %collective-permute-done.1.v_ref = bf16[2,256,256]{2,1,0:T(8,128)(2,1)S(1)} collective-permute-done((bf16[2,256,256]{2,1,0:T(8,128)(2,1)}, bf16[2,256,256]{2,1,0:T(8,128)(2,1)S(1)}, u32[]{:S(2)}, u32[]{:S(2)}) %collective-permute-start.1) | collective-permute-done | bytes 262176 | tf_op jit(solution)/shard_map/ppermute | solution.py:442
  26.3 0.0 collective-permute-done.2.first_ref
  26.3 14.6 %middle.1 = (f32[2,256,1792]{2,1,0:T(8,128)S(1)}, f32[2,256,1792]{2,1,0:T(8,128)S(1)}, f32[2,256,1792]{2,1,0:T(8,128)S(1)}) custom-call(s32[1]{0:T(128)} %bitcast.2.rank_ref, bf16[2,256,1792]{2,1,0:T(8,128)(2,1)S(1)} %get-tuple-element.26.q_ref.refs_0_, ...), custom_call_target="tpu_custom_call", output_to_operand_aliasing={{0}: (10, {}), {1}: (11, {}), {2}: (12, {})} | custom-call | flops 2348810240 | bytes 16000000 | tf_op jit(solution)/shard_map/middle/pallas_call | solution.py:522
  40.9 0.0 collective-permute-done.4.refs_6_
  40.9 6.5 %far.2.refs_7_ = bf16[2,256,1792]{2,1,0:T(8,128)(2,1)} custom-call(bf16[2,256,1792]{2,1,0:T(8,128)(2,1)S(1)} %get-tuple-element.26.q_ref.refs_0_, f32[2,256,1792]{2,1,0:T(8,128)S(1)} %get-tuple-element.40.refs_1_, f32[2,256,1792]{2,1,0:T(8,128)S(1)} %get-tuple-element.41.refs_2_, f32[2,256,1792]{2,1,0:T(8,128)S(1)} %get-tuple-element.42.refs_3_, ...), custom_call_target="tpu_custom_call" | custom-call | flops 469762048 | bytes 16000000 | tf_op jit(solution)/shard_map/far/pallas_call | solution.py:543
  47.4 0.0 collective-permute-done.3.refs_6_
  47.4 6.5 %far.3 = bf16[2,256,1792]{2,1,0:T(8,128)(2,1)} custom-call(bf16[2,256,1792]{2,1,0:T(8,128)(2,1)S(1)} %get-tuple-element.26.q_ref.refs_0_, f32[2,256,1792]{2,1,0:T(8,128)S(1)} %get-tuple-element.40.refs_1_, f32[2,256,1792]{2,1,0:T(8,128)S(1)} %get-tuple-element.41.refs_2_, ...), custom_call_target="tpu_custom_call", output_to_operand_aliasing={{}: (7, {})} | custom-call | flops 469762048 | bytes 16000000 | tf_op jit(solution)/shard_map/far/pallas_call | solution.py:543
Async XLA Ops:
  0.0 20.1 %collective-permute-start = (bf16[2,256,256]{2,1,0:T(8,128)(2,1)}, bf16[2,256,256]{2,1,0:T(8,128)(2,1)S(1)}, u32[]{:S(2)}, u32[]{:S(2)}) collective-permute-start(bf16[2,256,256]{2,1,0:T(8,128)(2,1)} %bitcast.8), channel_id=1, source_target_pairs={{0,4},{4,8},{8,12},{12,0},{1,5},{5,9},{9,13},{13,1},{2,6},{6,10},{... | collective-permute-start | bytes 786440 | tf_op jit(solution)/shard_map/ppermute | solution.py:442
  1.6 24.7 %collective-permute-start.1 = (bf16[2,256,256]{2,1,0:T(8,128)(2,1)}, bf16[2,256,256]{2,1,0:T(8,128)(2,1)S(1)}, u32[]{:S(2)}, u32[]{:S(2)}) collective-permute-start(bf16[2,256,256]{2,1,0:T(8,128)(2,1)} %bitcast.10), channel_id=1, source_target_pairs={{0,4},{4,8},{8,12},{12,0},{1,5},{5,9},{9,13},{13,1},{2,6},{6,10},{... | collective-permute-start | bytes 786440 | tf_op jit(solution)/shard_map/ppermute | solution.py:442
  1.8 0.9 %copy-start.1 = (bf16[1,2,256,256]{3,2,1,0:T(8,128)(2,1)S(1)}, bf16[1,2,256,256]{3,2,1,0:T(8,128)(2,1)}, u32[]{:S(2)}) copy-start(bf16[1,2,256,256]{3,2,1,0:T(8,128)(2,1)} %param.6) | copy-start | bytes 786436
  2.8 0.9 %copy-start.2 = (bf16[1,2,256,256]{3,2,1,0:T(8,128)(2,1)S(1)}, bf16[1,2,256,256]{3,2,1,0:T(8,128)(2,1)}, u32[]{:S(2)}) copy-start(bf16[1,2,256,256]{3,2,1,0:T(8,128)(2,1)} %param.7) | copy-start | bytes 786436
  3.7 0.7 %copy-start.3 = (s32[1,2,1024]{2,1,0:T(2,128)S(1)}, s32[1,2,1024]{2,1,0:T(2,128)}, u32[]{:S(2)}) copy-start(s32[1,2,1024]{2,1,0:T(2,128)} %param.8) | copy-start | bytes 24580
  6.0 20.3 %collective-permute-start.2 = (bf16[2,256,256]{2,1,0:T(8,128)(2,1)S(1)}, bf16[2,256,256]{2,1,0:T(8,128)(2,1)S(1)}, u32[]{:S(2)}, u32[]{:S(2)}) collective-permute-start(bf16[2,256,256]{2,1,0:T(8,128)(2,1)S(1)} %get-tuple-element.27), channel_id=1, source_target_pairs={{0,12},{4,0},{8,4},{12,8},{1,13},{5,1},{9,5},{13,9},{2,14},{6,2},{... | collective-permute-start | bytes 786440 | tf_op jit(solution)/shard_map/ppermute | solution.py:442
  7.8 1.5 %copy-start = (bf16[1,2,256,1792]{3,2,1,0:T(8,128)(2,1)S(1)}, bf16[1,2,256,1792]{3,2,1,0:T(8,128)(2,1)}, u32[]{:S(2)}) copy-start(bf16[1,2,256,1792]{3,2,1,0:T(8,128)(2,1)} %param.5) | copy-start | bytes 5505028
  9.3 0.7 %copy-start.4 = (s32[1,14,64]{2,0,1:T(1,128)S(1)}, s32[1,14,64]{2,0,1:T(1,128)}, u32[]{:S(2)}) copy-start(s32[1,14,64]{2,0,1:T(1,128)} %param.9) | copy-start | bytes 10756
  10.4 30.5 %collective-permute-start.4 = (bf16[2,256,128]{2,1,0:T(8,128)(2,1)S(1)}, bf16[2,256,128]{2,1,0:T(8,128)(2,1)S(1)}, u32[]{:S(2)}, u32[]{:S(2)}) collective-permute-start(bf16[2,256,128]{2,1,0:T(8,128)(2,1)S(1)} %get-tuple-element.44), channel_id=1, source_target_pairs={{0,8},{4,12},{8,0},{12,4},{1,9},{5,13},{9,1},{13,5},{2,10},{6,14},... | collective-permute-start | bytes 393224 | tf_op jit(solution)/shard_map/ppermute | solution.py:442
  19.2 28.2 %collective-permute-start.3 = (bf16[2,256,128]{2,1,0:T(8,128)(2,1)S(1)}, bf16[2,256,128]{2,1,0:T(8,128)(2,1)S(1)}, u32[]{:S(2)}, u32[]{:S(2)}) collective-permute-start(bf16[2,256,128]{2,1,0:T(8,128)(2,1)S(1)} %get-tuple-element.43), channel_id=1, source_target_pairs={{0,8},{4,12},{8,0},{12,4},{1,9},{5,13},{9,1},{13,5},{2,10},{6,14},... | collective-permute-start | bytes 393224 | tf_op jit(solution)/shard_map/ppermute | solution.py:442

commit v4 on v3

--- a/solution.py
+++ b/solution.py
@@ -156,14 +156,12 @@
     return pl.ds(pl.multiple_of(head * HEAD_SIZE, HEAD_SIZE), HEAD_SIZE)
 
 
-def split_keys(k_ref, v_ref, kv, rows, keys_ref, values_ref):
-    ones = jnp.ones((2 * rows, HEAD_SIZE), jnp.bfloat16)
-    for g in range(kv):
-        lanes = slice(g * HEAD_SIZE, (g + 1) * HEAD_SIZE)
-        for ref, to in ((k_ref, keys_ref), (v_ref, values_ref)):
-            to[g, :rows, :HEAD_SIZE] = ref[0, :, lanes]
-            to[g, rows:, :HEAD_SIZE] = ref[1, :, lanes]
-        values_ref[g, :, HEAD_SIZE:] = ones
+def split_keys(k_ref, v_ref, g, rows, keys_ref, values_ref):
+    lanes = slice(g * HEAD_SIZE, (g + 1) * HEAD_SIZE)
+    for ref, to in ((k_ref, keys_ref), (v_ref, values_ref)):
+        to[:rows, :HEAD_SIZE] = ref[0, :, lanes]
+        to[rows:, :HEAD_SIZE] = ref[1, :, lanes]
+    values_ref[:, HEAD_SIZE:] = jnp.ones((2 * rows, HEAD_SIZE), jnp.bfloat16)
 
 
 def slash_blocks(slash_ref, head, t):
@@ -196,84 +194,83 @@
         slash_ref[head, :, rows:] = jnp.full((1, rows), DEAD, jnp.float32)
 
 
-def hold_kernel(rows, heads, late, offsets_ref, q_ref, *refs):
-    slash_ref, qcopy_ref = refs[late : late + 2]
+def slash_kernel(rows, heads, offsets_ref, q_ref, slash_ref, qcopy_ref):
     make_slash(offsets_ref, slash_ref, rows, heads)
     qcopy_ref[...] = q_ref[...]
-    for a, b in zip(refs[:late], refs[late + 2 :]):
-        b[...] = a[...]
 
 
 def own_kernel(
-    rows, kv, group_size,
+    rows, g, group_size,
     q_ref, k_ref, v_ref, band_bias_ref, extra_bias_ref, slash_ref, *refs,
 ):
-    passed = (len(refs) - 8) // 2
-    for a, b in zip(refs[:passed], refs[passed + 5 :]):
+    if g:
+        gauge_in, *refs = refs
+    *sent, acc_ref, sum_ref, shift_ref, gauge_ref, table_ref, held = refs[:-3]
+    keys_ref, values_ref, tri_ref = refs[-3:]
+    for a, b in zip(sent, held):
         b[...] = a[...]
-    acc_ref, sum_ref, shift_ref, gauge_ref, table_ref = refs[passed : passed + 5]
-    keys_ref, values_ref, tri_ref = refs[-3:]
     t = rows // 2
     tri = lax.broadcasted_iota(jnp.int32, (t, t), 0) >= lax.broadcasted_iota(jnp.int32, (t, t), 1)
-    split_keys(k_ref, v_ref, kv, rows, keys_ref, values_ref)
-    for g in range(kv):
+    split_keys(k_ref, v_ref, g, rows, keys_ref, values_ref)
+    for m in range(2):
+        for b in range(2):
+            row = band_bias_ref[g, m : m + 1, rows + b * t : rows + (b + 1) * t]
+            tri_ref[m, b] = jnp.where(tri, row, DEAD)
+
+    if g:
+        gauge_ref[...] = gauge_in[...]
+    else:
+        gauge_ref[0] = jnp.zeros((8, HEAD_SIZE), jnp.float32)
+        gauge_ref[1] = jnp.full((8, HEAD_SIZE), -DEAD, jnp.float32)
+    blank = jnp.zeros((t, t), jnp.bfloat16)
+    def one_head(h, carry):
+        head = g * group_size + h
+        at = lanes_of(h)
+        t2, t1, t0 = slash_blocks(slash_ref, head, t)
+        table_ref[h, :, :t] = t2
+        table_ref[h, :, t:] = t1
         for m in range(2):
-            for b in range(2):
-                row = band_bias_ref[g, m : m + 1, rows + b * t : rows + (b + 1) * t]
-                tri_ref[g, m, b] = jnp.where(tri, row, DEAD)
-
-    gauge_ref[0] = jnp.zeros((8, HEAD_SIZE), jnp.float32)
-    gauge_ref[1] = jnp.full((8, HEAD_SIZE), -DEAD, jnp.float32)
-    blank = jnp.zeros((t, t), jnp.bfloat16)
-    for g in range(kv):
-
-        def one_head(h, carry):
-            head = g * group_size + h
-            at = lanes_of(head)
-            t2, t1, t0 = slash_blocks(slash_ref, head, t)
-            table_ref[head, :, :t] = t2
-            table_ref[head, :, t:] = t1
-            for m in range(2):
-                q = q_ref[m, :, at]
-                s = dot_nt(q, keys_ref[g, : (m + 1) * rows]) * SCALE2
-                band = s[:, m * rows :]
-                row = band_bias_ref[g, m : m + 1, rows : rows + t]
-                top = [band[:t, :t] + jnp.maximum(t0, tri_ref[g, m, 0])]
-                low = [
-                    band[t:, :t] + jnp.maximum(t1, row),
-                    band[t:, t:] + jnp.maximum(t0, tri_ref[g, m, 1]),
-                ]
-                if m == 1:
-                    more = columns_of(s[:, :rows] + extra_bias_ref[g, :, :rows], 2)
-                    top = [x[:t] for x in more] + top
-                    low = [x[t:] for x in more] + low
-                top_shift, low_shift = row_max(top), row_max(low)
-                p = jnp.concatenate(
-                    [
-                        jnp.concatenate(weights_of(top, top_shift) + [blank], axis=1),
-                        jnp.concatenate(weights_of(low, low_shift), axis=1),
-                    ],
-                    axis=0,
-                )
-                o = dot_nn(p, values_ref[g, : (m + 1) * rows])
-                shift = jnp.concatenate([top_shift, low_shift], axis=0)
-                acc_ref[m, :, at] = o[:, :HEAD_SIZE]
-                sum_ref[m, :, at] = o[:, HEAD_SIZE:]
-                shift_ref[m, :, at] = shift
-                gauge_ref[0] = jnp.maximum(gauge_ref[0], folded(norms(q), jnp.maximum))
-                gauge_ref[1] = jnp.minimum(gauge_ref[1], folded(shift, jnp.minimum))
-            return carry
-
-        lax.fori_loop(0, group_size, one_head, 0, unroll=True)
+            q = q_ref[m, :, lanes_of(head)]
+            s = dot_nt(q, keys_ref[: (m + 1) * rows]) * SCALE2
+            band = s[:, m * rows :]
+            row = band_bias_ref[g, m : m + 1, rows : rows + t]
+            top = [band[:t, :t] + jnp.maximum(t0, tri_ref[m, 0])]
+            low = [
+                band[t:, :t] + jnp.maximum(t1, row),
+                band[t:, t:] + jnp.maximum(t0, tri_ref[m, 1]),
+            ]
+            if m == 1:
+                more = columns_of(s[:, :rows] + extra_bias_ref[g, :, :rows], 2)
+                top = [x[:t] for x in more] + top
+                low = [x[t:] for x in more] + low
+            top_shift, low_shift = row_max(top), row_max(low)
+            p = jnp.concatenate(
+                [
+                    jnp.concatenate(weights_of(top, top_shift) + [blank], axis=1),
+                    jnp.concatenate(weights_of(low, low_shift), axis=1),
+                ],
+                axis=0,
+            )
+            o = dot_nn(p, values_ref[: (m + 1) * rows])
+            shift = jnp.concatenate([top_shift, low_shift], axis=0)
+            acc_ref[m, :, at] = o[:, :HEAD_SIZE]
+            sum_ref[m, :, at] = o[:, HEAD_SIZE:]
+            shift_ref[m, :, at] = shift
+            gauge_ref[0] = jnp.maximum(gauge_ref[0], folded(norms(q), jnp.maximum))
+            gauge_ref[1] = jnp.minimum(gauge_ref[1], folded(shift, jnp.minimum))
+        return carry
+
+    lax.fori_loop(0, group_size, one_head, 0, unroll=True)
 
 
 def middle_kernel(
     rows, kv, group_size,
-    rank_ref, q_ref, k_ref, v_ref, first_ref, band_bias_ref, extra_bias_ref, remote_bias_ref,
-    table_ref, gauge_ref, acc_in, sum_in, shift_in,
-    acc_ref, sum_ref, shift_ref,
-    keys_ref, values_ref,
+    rank_ref, q_ref, k_ref, v_ref, first_ref, band_bias_ref, extra_bias_ref, remote_bias_ref, *refs,
 ):
+    acc_in, sum_in, shift_in, tables, gauges, acc_ref, sum_ref, shift_ref = (
+        refs[i * kv : (i + 1) * kv] for i in range(8)
+    )
+    keys_ref, values_ref = refs[-2:]
     first_rank = rank_ref[0] == 0
     shut = jnp.where(first_rank, DEAD, 0.0)
     t = rows // 2
@@ -290,10 +287,10 @@
         for part in range(3):
             k = keys_ref[g, part * rows : (part + 1) * rows]
             key_norm = jnp.maximum(key_norm, folded(norms(k), jnp.maximum))
-    fast = in_range(gauge_ref[0], key_norm, gauge_ref[1])
-
-    def scores(g, m, head, q):
-        t2, t1 = table_ref[head, :, :t], table_ref[head, :, t:]
+    fast = in_range(gauges[-1][0], key_norm, gauges[-1][1])
+
+    def scores(g, m, h, q):
+        t2, t1 = tables[g][h, :, :t], tables[g][h, :, t:]
         if m == 0:
             t2, t1 = t2 + shut, t1 + shut
         s = dot_nt(q, keys_ref[g, (1 - m) * rows :]) * SCALE2
@@ -318,23 +315,22 @@
     def merge(g, m, at, blocks, shift, shrink):
         p = jnp.concatenate(weights_of(blocks, shift), axis=1)
         o = dot_nn(p, values_ref[g, (1 - m) * rows :])
-        acc, total = acc_in[m, :, at], sum_in[m, :, at]
+        acc, total = acc_in[g][m, :, at], sum_in[g][m, :, at]
         if shrink is not None:
             acc, total = acc * shrink, total * shrink
-        acc_ref[m, :, at] = acc + o[:, :HEAD_SIZE]
-        sum_ref[m, :, at] = total + o[:, HEAD_SIZE:]
+        acc_ref[g][m, :, at] = acc + o[:, :HEAD_SIZE]
+        sum_ref[g][m, :, at] = total + o[:, HEAD_SIZE:]
 
     @pl.when(fast)
     def _():
         for g in range(kv):
 
             def one_head(h, carry):
-                head = g * group_size + h
-                at = lanes_of(head)
+                at, from_q = lanes_of(h), lanes_of(g * group_size + h)
                 for m in range(2):
-                    shift = shift_in[m, :, at]
-                    merge(g, m, at, scores(g, m, head, q_ref[m, :, at]), shift, None)
-                    shift_ref[m, :, at] = shift
+                    shift = shift_in[g][m, :, at]
+                    merge(g, m, at, scores(g, m, h, q_ref[m, :, from_q]), shift, None)
+                    shift_ref[g][m, :, at] = shift
                 return carry
 
             lax.fori_loop(0, group_size, one_head, 0, unroll=True)
@@ -344,22 +340,21 @@
         for g in range(kv):
 
             def one_head(h, carry):
-                head = g * group_size + h
-                at = lanes_of(head)
+                at, from_q = lanes_of(h), lanes_of(g * group_size + h)
                 for m in range(2):
-                    blocks = scores(g, m, head, q_ref[m, :, at])
-                    old = shift_in[m, :, at]
+                    blocks = scores(g, m, h, q_ref[m, :, from_q])
+                    old = shift_in[g][m, :, at]
                     shift = jnp.maximum(old, row_max(blocks))
                     merge(g, m, at, blocks, shift, jnp.exp2(old - shift))
-                    shift_ref[m, :, at] = shift
+                    shift_ref[g][m, :, at] = shift
                 return carry
 
             lax.fori_loop(0, group_size, one_head, 0)
 
 
 def far_kernel(rows, g, group_size, count, *refs):
-    q_ref, acc_ref, sum_ref, shift_ref, gauge_ref, remote_bias_ref = refs[:6]
-    arrived = refs[6 : 6 + count]
+    rank_ref, q_ref, acc_ref, sum_ref, shift_ref, gauge_ref, remote_bias_ref = refs[:7]
+    arrived = refs[7 : 7 + count]
     out_hbm, keys_ref, values_ref, out_ref, sems = refs[-5:]
     ones = jnp.ones((rows, HEAD_SIZE), jnp.bfloat16)
     key_norm = jnp.zeros((8, HEAD_SIZE), jnp.float32)
@@ -391,20 +386,28 @@
         out = (acc + o[:, :HEAD_SIZE]) / (total + o[:, HEAD_SIZE:])
         out_ref[h, m] = out.astype(jnp.bfloat16)
 
-    for h in range(group_size):
-        at = lanes_of(g * group_size + h)
-        for m in range(2):
-            finish(h, m, at, scores(m, q_ref[m, :, at]), shift_ref[m, :, at], None)
-        copies[h].start()
-    for copy in copies:
-        copy.wait()
+    def attend(first_half):
+        for h in range(group_size):
+            at, from_q = lanes_of(h), lanes_of(g * group_size + h)
+            if first_half:
+                finish(h, 0, at, scores(0, q_ref[0, :, from_q]), shift_ref[0, :, at], None)
+            else:
+                out_ref[h, 0] = (acc_ref[0, :, at] / sum_ref[0, :, at]).astype(jnp.bfloat16)
+            finish(h, 1, at, scores(1, q_ref[1, :, from_q]), shift_ref[1, :, at], None)
+            copies[h].start()
+        for copy in copies:
+            copy.wait()
+
+    sees = rank_ref[0] >= 2
+    pl.when(sees)(lambda: attend(True))
+    pl.when(jnp.logical_not(sees))(lambda: attend(False))
 
     @pl.when(jnp.logical_not(fast))
     def _():
         def one_head(h, carry):
-            at = lanes_of(g * group_size + h)
+            at, from_q = lanes_of(h), lanes_of(g * group_size + h)
             for m in range(2):
-                blocks = scores(m, q_ref[m, :, at])
+                blocks = scores(m, q_ref[m, :, from_q])
                 old = shift_ref[m, :, at]
                 shift = jnp.maximum(old, row_max(blocks))
                 finish(h, m, at, blocks, shift, jnp.exp2(old - shift))
@@ -469,9 +472,7 @@
     whole, band_bias, extra_bias, remote_bias, kv_k, kv_v = prepared[late * kv :]
     first = shifted(whole, n - 1)
 
-    state = jax.ShapeDtypeStruct((2, rows, heads * HEAD_SIZE), jnp.float32)
-    keys_scratch = pltpu.VMEM((kv, 2 * rows, HEAD_SIZE), jnp.bfloat16)
-    values_scratch = pltpu.VMEM((kv, 2 * rows, 2 * HEAD_SIZE), jnp.bfloat16)
+    state = jax.ShapeDtypeStruct((2, rows, group_size * HEAD_SIZE), jnp.float32)
 
     def cost(blocks):
         return pl.CostEstimate(
@@ -480,61 +481,62 @@
             transcendentals=heads * blocks * rows * rows,
         )
 
-    slash, qv, *held = pl.pallas_call(
-        functools.partial(hold_kernel, rows, heads, late),
+    slash, qv = pl.pallas_call(
+        functools.partial(slash_kernel, rows, heads),
         out_shape=[
             jax.ShapeDtypeStruct((heads, 1, 2 * rows), jnp.float32),
             jax.ShapeDtypeStruct(q.shape, q.dtype),
-        ]
-        + [piece] * late,
-        in_specs=[vmem] * (2 + late),
-        out_specs=[vmem] * (2 + late),
+        ],
+        in_specs=[vmem] * 2,
+        out_specs=[vmem] * 2,
         compiler_params=params,
-        name="hold",
-    )(offsets, q, *pieces[::kv])
-    arrived = [[shifted(x, i + 2) for i, x in enumerate(held)]]
-
-    rest = [x for i, x in enumerate(pieces) if i % kv]
-    acc, total, shift, gauge, table, *rest = pl.pallas_call(
-        functools.partial(own_kernel, rows, kv, group_size),
-        out_shape=[
-            state,
-            state,
-            state,
-            jax.ShapeDtypeStruct((2, 8, HEAD_SIZE), jnp.float32),
-            jax.ShapeDtypeStruct((heads, rows // 2, rows), jnp.float32),
-        ]
-        + [piece] * len(rest),
-        in_specs=[vmem] * (6 + len(rest)),
-        out_specs=[vmem] * (5 + len(rest)),
-        scratch_shapes=[
-            keys_scratch,
-            values_scratch,
-            pltpu.VMEM((kv, 2, 2, rows // 2, rows // 2), jnp.float32),
-        ],
-        compiler_params=params,
-        cost_estimate=cost(3),
-        name="own",
-    )(qv, kv_k, kv_v, band_bias, extra_bias, slash, *rest)
-    for g in range(kv - 1):
-        arrived.append([shifted(x, i + 2) for i, x in enumerate(rest[g :: kv - 1])])
-
-    acc, total, shift = pl.pallas_call(
+        name="slash",
+    )(offsets, q)
+
+    made, arrived = [], []
+    for g in range(kv):
+        sent = [x[3] for x in made[-1:]] + list(pieces[g::kv])
+        *own, held = pl.pallas_call(
+            functools.partial(own_kernel, rows, g, group_size),
+            out_shape=[
+                state,
+                state,
+                state,
+                jax.ShapeDtypeStruct((2, 8, HEAD_SIZE), jnp.float32),
+                jax.ShapeDtypeStruct((group_size, rows // 2, rows), jnp.float32),
+                [piece] * late,
+            ],
+            in_specs=[vmem] * (6 + len(sent)),
+            out_specs=[vmem] * 5 + [[vmem] * late],
+            scratch_shapes=[
+                pltpu.VMEM((2 * rows, HEAD_SIZE), jnp.bfloat16),
+                pltpu.VMEM((2 * rows, 2 * HEAD_SIZE), jnp.bfloat16),
+                pltpu.VMEM((2, 2, rows // 2, rows // 2), jnp.float32),
+            ],
+            compiler_params=params,
+            cost_estimate=cost(2),
+            name="own",
+        )(qv, kv_k, kv_v, band_bias, extra_bias, slash, *sent)
+        made.append(own)
+        arrived.append([shifted(x, i + 2) for i, x in enumerate(held)])
+    accs, totals, shifts, gauges, tables = zip(*made)
+
+    states = pl.pallas_call(
         functools.partial(middle_kernel, rows, kv, group_size),
-        out_shape=[state] * 3,
-        in_specs=[smem] + [vmem] * 12,
-        out_specs=[vmem] * 3,
+        out_shape=[state] * (3 * kv),
+        in_specs=[smem] + [vmem] * (7 + 5 * kv),
+        out_specs=[vmem] * (3 * kv),
         scratch_shapes=[
             pltpu.VMEM((kv, 3 * rows, HEAD_SIZE), jnp.bfloat16),
             pltpu.VMEM((kv, 3 * rows, 2 * HEAD_SIZE), jnp.bfloat16),
         ],
-        input_output_aliases={10: 0, 11: 1, 12: 2},
+        input_output_aliases={8 + i: i for i in range(3 * kv)},
         compiler_params=params,
         cost_estimate=cost(5),
         name="middle",
     )(
-        rank1, qv, k_before, v_before, first, band_bias, extra_bias, remote_bias, table, gauge,
-        acc, total, shift,
+        rank1, qv, k_before, v_before, first, band_bias, extra_bias, remote_bias,
+        *accs, *totals, *shifts, *tables, *gauges,
     )
 
     out = []
@@ -543,7 +545,7 @@
             pl.pallas_call(
                 functools.partial(far_kernel, rows, g, group_size, late),
                 out_shape=jax.ShapeDtypeStruct(q.shape, jnp.bfloat16),
-                in_specs=[vmem] * (6 + late) + [hbm] * len(out),
+                in_specs=[smem] + [vmem] * (6 + late) + [hbm] * len(out),
                 out_specs=hbm,
                 scratch_shapes=[
                     pltpu.VMEM((late * rows, HEAD_SIZE), jnp.bfloat16),
@@ -551,11 +553,11 @@
                     pltpu.VMEM((group_size, 2, rows, HEAD_SIZE), jnp.bfloat16),
                     pltpu.SemaphoreType.DMA((group_size,)),
                 ],
-                input_output_aliases={6 + late: 0} if out else {},
+                input_output_aliases={7 + late: 0} if out else {},
                 compiler_params=params,
                 cost_estimate=cost(late),
                 name="far",
-            )(qv, acc, total, shift, gauge, remote_bias, *arrived[g], *out)
+            )(rank1, qv, *states[g::kv], gauges[g], remote_bias, *arrived[g], *out)
         ]
     return out[0][None]
 

time: 54.4 us -> 52.2 us (0.960)
  waiting for transfers between devices: 6.21 us -> 3.28 us
  Pallas kernels: 36.2 us -> 36.9 us
    ppermute x5, waiting for transfers between devices: 6.21 us -> 3.28 us  [shifted(): return lax.ppermute(x, 'ctx', [(i, (i + d) % n) for i in range(n)])]
    pallas_call x2 -> x3, Pallas kernels: 6.98 us -> 7.37 us  [the longest x2 7.01 us: per_device(): pl.pallas_call(functools.partial(own_kernel, rows, g, group_size), out_sh...]
  transfers between devices with their start and end apart: 5 -> 5, of which waited for: 1 -> 1; matrix products, arithmetic and copies ran while one was open for 0% -> 0% of each run, Pallas kernels for 55% -> 58%
where the time goes in v4:
time: 52.2 us; the launch traced here: 51.9 us
  Pallas kernels  36.9 us (71%)
  starting transfers between devices  6.71 us (13%)
  local copies, waits for them, and re-layouts  4.79 us (9%)
  waiting for transfers between devices  3.28 us (6%)
    pallas_call x1, Pallas kernels, per_device(): pl.pallas_call(functools.partial(middle_kernel, rows, kv, group_size), ou...  14.6 us
    pallas_call x2, Pallas kernels, per_device(): pl.pallas_call(functools.partial(far_kernel, rows, g, group_size, late),...  13.4 us
    pallas_call x2, Pallas kernels, per_device(): pl.pallas_call(functools.partial(own_kernel, rows, g, group_size), out_sh...  7.01 us
    ppermute x5, starting transfers between devices, shifted(): return lax.ppermute(x, 'ctx', [(i, (i + d) % n) for i in range(n)])  6.71 us
    unnamed x10, local copies, waits for them, and re-layouts  4.79 us
    ppermute x5, waiting for transfers between devices, shifted(): return lax.ppermute(x, 'ctx', [(i, (i + d) % n) for i in range(n)])  3.28 us
    pallas_call x1, Pallas kernels, per_device(): pl.pallas_call(functools.partial(prep_kernel, n, rows, kv), out_shape=[pi...  1.55 us
  transfers between devices with their start and end apart: 5, of which 1 were waited for; matrix products, arithmetic and copies ran while one was open for 0% of the time, Pallas kernels for 58%

profile of v4, /device:TPU:18, one launch (start us, length us, event | category | flops | bytes accessed | tf_op | source)
XLA Modules:
  0.0 51.9 jit_solution(3558058906415492715)
XLA Ops:
  0.0 1.6 %collective-permute-start = (bf16[2,256,256]{2,1,0:T(8,128)(2,1)}, bf16[2,256,256]{2,1,0:T(8,128)(2,1)S(1)}, u32[]{:S(2)}, u32[]{:S(2)}) collective-permute-start(bf16[2,256,256]{2,1,0:T(8,128)(2,1)} %bitcast.8), channel_id=1, source_target_pairs={{0,4},{4,8},{8,12},{12,0},{1,5},{5,9},{9,13},{13,1},{2,6},{6,10},{... | collective-permute-start | bytes 786440 | tf_op jit(solution)/shard_map/ppermute | solution.py:445
  1.6 0.2 collective-permute-start.1
  1.8 0.0 copy-start.1
  1.8 0.9 %copy-done.1 = bf16[1,2,256,256]{3,2,1,0:T(8,128)(2,1)S(1)} copy-done((bf16[1,2,256,256]{3,2,1,0:T(8,128)(2,1)S(1)}, bf16[1,2,256,256]{3,2,1,0:T(8,128)(2,1)}, u32[]{:S(2)}) %copy-start.1) | copy-done | bytes 262168
  2.8 0.0 copy-start.2
  2.8 0.9 %copy-done.2 = bf16[1,2,256,256]{3,2,1,0:T(8,128)(2,1)S(1)} copy-done((bf16[1,2,256,256]{3,2,1,0:T(8,128)(2,1)S(1)}, bf16[1,2,256,256]{3,2,1,0:T(8,128)(2,1)}, u32[]{:S(2)}) %copy-start.2) | copy-done | bytes 262168
  3.7 0.0 copy-start.3
  3.7 0.7 %copy-done.3 = s32[1,2,1024]{2,1,0:T(2,128)S(1)} copy-done((s32[1,2,1024]{2,1,0:T(2,128)S(1)}, s32[1,2,1024]{2,1,0:T(2,128)}, u32[]{:S(2)}) %copy-start.3) | copy-done | bytes 8216
  4.4 1.5 %prep.1 = (bf16[2,256,128]{2,1,0:T(8,128)(2,1)S(1)}, bf16[2,256,128]{2,1,0:T(8,128)(2,1)S(1)}, bf16[2,256,256]{2,1,0:T(8,128)(2,1)S(1)}, f32[2,2,512]{2,1,0:T(2,...) custom-call(s32[1]{0:T(128)} %bitcast.rank_ref.refs_0_, ...), custom_call_target="tpu_custom_call" | custom-call | tf_op jit(solution)/shard_map/prep/pallas_call | solution.py:449
  6.0 1.9 %collective-permute-start.2 = (bf16[2,256,256]{2,1,0:T(8,128)(2,1)S(1)}, bf16[2,256,256]{2,1,0:T(8,128)(2,1)S(1)}, u32[]{:S(2)}, u32[]{:S(2)}) collective-permute-start(bf16[2,256,256]{2,1,0:T(8,128)(2,1)S(1)} %get-tuple-element.34), channel_id=1, source_target_pairs={{0,12},{4,0},{8,4},{12,8},{1,13},{5,1},{9,5},{13,9},{2,14},{6,2},{... | collective-permute-start | bytes 786440 | tf_op jit(solution)/shard_map/ppermute | solution.py:445
  7.8 0.0 copy-start
  7.8 1.5 %copy-done = bf16[1,2,256,1792]{3,2,1,0:T(8,128)(2,1)S(1)} copy-done((bf16[1,2,256,1792]{3,2,1,0:T(8,128)(2,1)S(1)}, bf16[1,2,256,1792]{3,2,1,0:T(8,128)(2,1)}, u32[]{:S(2)}) %copy-start) | copy-done | bytes 1835032
  9.3 0.0 copy-start.4
  9.3 0.7 %copy-done.4 = s32[1,14,64]{2,0,1:T(1,128)S(1)} copy-done((s32[1,14,64]{2,0,1:T(1,128)S(1)}, s32[1,14,64]{2,0,1:T(1,128)}, u32[]{:S(2)}) %copy-start.4) | copy-done | bytes 3608
  10.0 0.4 slash.1
  10.4 3.5 %own.2 = (f32[2,256,896]{2,1,0:T(8,128)S(1)}, f32[2,256,896]{2,1,0:T(8,128)S(1)}, f32[2,256,896]{2,1,0:T(8,128)S(1)}, f32[2,8,128]{2,1,0:T(8,128)S(1)}, f32[7,12...) custom-call(bf16[2,256,1792]{2,1,0:T(8,128)(2,1)S(1)} %get-tuple-element.33.q_ref.refs_1_, ...), custom_call_target="tpu_custom_call" | custom-call | flops 939524096 | bytes 16000000 | tf_op jit(solution)/shard_map/own/pallas_call | solution.py:499
  13.9 2.2 %collective-permute-start.4 = (bf16[2,256,128]{2,1,0:T(8,128)(2,1)S(1)}, bf16[2,256,128]{2,1,0:T(8,128)(2,1)S(1)}, u32[]{:S(2)}, u32[]{:S(2)}) collective-permute-start(bf16[2,256,128]{2,1,0:T(8,128)(2,1)S(1)} %get-tuple-element.60), channel_id=1, source_target_pairs={{0,8},{4,12},{8,0},{12,4},{1,9},{5,13},{9,1},{13,5},{2,10},{6,14},... | collective-permute-start | bytes 393224 | tf_op jit(solution)/shard_map/ppermute | solution.py:445
  16.1 3.5 %own.3 = (f32[2,256,896]{2,1,0:T(8,128)S(1)}, f32[2,256,896]{2,1,0:T(8,128)S(1)}, f32[2,256,896]{2,1,0:T(8,128)S(1)}, f32[2,8,128]{2,1,0:T(8,128)S(1)}, f32[7,12...) custom-call(bf16[2,256,1792]{2,1,0:T(8,128)(2,1)S(1)} %get-tuple-element.33.q_ref.refs_1_, ...), custom_call_target="tpu_custom_call" | custom-call | flops 939524096 | bytes 16000000 | tf_op jit(solution)/shard_map/own/pallas_call | solution.py:499
  19.6 0.9 %collective-permute-start.3 = (bf16[2,256,128]{2,1,0:T(8,128)(2,1)S(1)}, bf16[2,256,128]{2,1,0:T(8,128)(2,1)S(1)}, u32[]{:S(2)}, u32[]{:S(2)}) collective-permute-start(bf16[2,256,128]{2,1,0:T(8,128)(2,1)S(1)} %get-tuple-element.56), channel_id=1, source_target_pairs={{0,8},{4,12},{8,0},{12,4},{1,9},{5,13},{9,1},{13,5},{2,10},{6,14},... | collective-permute-start | bytes 393224 | tf_op jit(solution)/shard_map/ppermute | solution.py:445
  20.4 0.0 collective-permute-done.k_ref
  20.4 3.3 %collective-permute-done.1.v_ref = bf16[2,256,256]{2,1,0:T(8,128)(2,1)S(1)} collective-permute-done((bf16[2,256,256]{2,1,0:T(8,128)(2,1)}, bf16[2,256,256]{2,1,0:T(8,128)(2,1)S(1)}, u32[]{:S(2)}, u32[]{:S(2)}) %collective-permute-start.1) | collective-permute-done | bytes 262176 | tf_op jit(solution)/shard_map/ppermute | solution.py:445
  23.7 0.0 collective-permute-done.2.first_ref
  23.7 14.6 %middle.1 = (f32[2,256,896]{2,1,0:T(8,128)S(1)}, f32[2,256,896]{2,1,0:T(8,128)S(1)}, f32[2,256,896]{2,1,0:T(8,128)S(1)}, f32[2,256,896]{2,1,0:T(8,128)S(1)}, f32...) custom-call(s32[1]{0:T(128)} %bitcast.rank_ref.refs_0_, ...), custom_call_target="tpu_custom_call", output_to_operand_aliasing={{0}: (8, {}), {1}: (9, {}), {2}: (10, {}), {3}: (11, {}), {... | custom-call | flops 2348810240 | bytes 16000000 | tf_op jit(solution)/shard_map/middle/pallas_call | solution.py:524
  38.3 0.0 collective-permute-done.4.refs_7_
  38.3 6.7 %far.2.refs_8_ = bf16[2,256,1792]{2,1,0:T(8,128)(2,1)} custom-call(s32[1]{0:T(128)} %bitcast.rank_ref.refs_0_, bf16[2,256,1792]{2,1,0:T(8,128)(2,1)S(1)} %get-tuple-element.33.q_ref.refs_1_, f32[2,256,896]{2,1,0:T(8,128)S(1)} %get-tuple-element.57.refs_2_, f32[2,256,896]{2,1,0:T(8,128)S(1)} %get-tuple-element.58.refs_3_, ...), custom_call_target="tpu_custom_call" | custom-call | flops 469762048 | bytes 16000000 | tf_op jit(solution)/shard_map/far/pallas_call | solution.py:545
  45.0 0.0 collective-permute-done.3.refs_7_
  45.0 6.7 %far.3 = bf16[2,256,1792]{2,1,0:T(8,128)(2,1)} custom-call(s32[1]{0:T(128)} %bitcast.rank_ref.refs_0_, bf16[2,256,1792]{2,1,0:T(8,128)(2,1)S(1)} %get-tuple-element.33.q_ref.refs_1_, f32[2,256,896]{2,1,0:T(8,128)S(1)} %get-tuple-element.53.refs_2_, f32[2,256,896]{2,1,0:T(8,128)S(1)} %get-tuple-element.54.refs_3_, ...), custom_call_target="tpu_custom_call", output_to_operand_aliasing={{}: (8, {})} | custom-call | flops 469762048 | bytes 16000000 | tf_op jit(solution)/shard_map/far/pallas_call | solution.py:545
Async XLA Ops:
  0.0 20.4 %collective-permute-start = (bf16[2,256,256]{2,1,0:T(8,128)(2,1)}, bf16[2,256,256]{2,1,0:T(8,128)(2,1)S(1)}, u32[]{:S(2)}, u32[]{:S(2)}) collective-permute-start(bf16[2,256,256]{2,1,0:T(8,128)(2,1)} %bitcast.8), channel_id=1, source_target_pairs={{0,4},{4,8},{8,12},{12,0},{1,5},{5,9},{9,13},{13,1},{2,6},{6,10},{... | collective-permute-start | bytes 786440 | tf_op jit(solution)/shard_map/ppermute | solution.py:445
  1.6 22.1 %collective-permute-start.1 = (bf16[2,256,256]{2,1,0:T(8,128)(2,1)}, bf16[2,256,256]{2,1,0:T(8,128)(2,1)S(1)}, u32[]{:S(2)}, u32[]{:S(2)}) collective-permute-start(bf16[2,256,256]{2,1,0:T(8,128)(2,1)} %bitcast.10), channel_id=1, source_target_pairs={{0,4},{4,8},{8,12},{12,0},{1,5},{5,9},{9,13},{13,1},{2,6},{6,10},{... | collective-permute-start | bytes 786440 | tf_op jit(solution)/shard_map/ppermute | solution.py:445
  1.8 0.9 %copy-start.1 = (bf16[1,2,256,256]{3,2,1,0:T(8,128)(2,1)S(1)}, bf16[1,2,256,256]{3,2,1,0:T(8,128)(2,1)}, u32[]{:S(2)}) copy-start(bf16[1,2,256,256]{3,2,1,0:T(8,128)(2,1)} %param.6) | copy-start | bytes 786436
  2.8 0.9 %copy-start.2 = (bf16[1,2,256,256]{3,2,1,0:T(8,128)(2,1)S(1)}, bf16[1,2,256,256]{3,2,1,0:T(8,128)(2,1)}, u32[]{:S(2)}) copy-start(bf16[1,2,256,256]{3,2,1,0:T(8,128)(2,1)} %param.7) | copy-start | bytes 786436
  3.7 0.7 %copy-start.3 = (s32[1,2,1024]{2,1,0:T(2,128)S(1)}, s32[1,2,1024]{2,1,0:T(2,128)}, u32[]{:S(2)}) copy-start(s32[1,2,1024]{2,1,0:T(2,128)} %param.8) | copy-start | bytes 24580
  6.0 17.8 %collective-permute-start.2 = (bf16[2,256,256]{2,1,0:T(8,128)(2,1)S(1)}, bf16[2,256,256]{2,1,0:T(8,128)(2,1)S(1)}, u32[]{:S(2)}, u32[]{:S(2)}) collective-permute-start(bf16[2,256,256]{2,1,0:T(8,128)(2,1)S(1)} %get-tuple-element.34), channel_id=1, source_target_pairs={{0,12},{4,0},{8,4},{12,8},{1,13},{5,1},{9,5},{13,9},{2,14},{6,2},{... | collective-permute-start | bytes 786440 | tf_op jit(solution)/shard_map/ppermute | solution.py:445
  7.8 1.5 %copy-start = (bf16[1,2,256,1792]{3,2,1,0:T(8,128)(2,1)S(1)}, bf16[1,2,256,1792]{3,2,1,0:T(8,128)(2,1)}, u32[]{:S(2)}) copy-start(bf16[1,2,256,1792]{3,2,1,0:T(8,128)(2,1)} %param.5) | copy-start | bytes 5505028
  9.3 0.7 %copy-start.4 = (s32[1,14,64]{2,0,1:T(1,128)S(1)}, s32[1,14,64]{2,0,1:T(1,128)}, u32[]{:S(2)}) copy-start(s32[1,14,64]{2,0,1:T(1,128)} %param.9) | copy-start | bytes 10756
  13.9 24.4 %collective-permute-start.4 = (bf16[2,256,128]{2,1,0:T(8,128)(2,1)S(1)}, bf16[2,256,128]{2,1,0:T(8,128)(2,1)S(1)}, u32[]{:S(2)}, u32[]{:S(2)}) collective-permute-start(bf16[2,256,128]{2,1,0:T(8,128)(2,1)S(1)} %get-tuple-element.60), channel_id=1, source_target_pairs={{0,8},{4,12},{8,0},{12,4},{1,9},{5,13},{9,1},{13,5},{2,10},{6,14},... | collective-permute-start | bytes 393224 | tf_op jit(solution)/shard_map/ppermute | solution.py:445
  19.6 25.4 %collective-permute-start.3 = (bf16[2,256,128]{2,1,0:T(8,128)(2,1)S(1)}, bf16[2,256,128]{2,1,0:T(8,128)(2,1)S(1)}, u32[]{:S(2)}, u32[]{:S(2)}) collective-permute-start(bf16[2,256,128]{2,1,0:T(8,128)(2,1)S(1)} %get-tuple-element.56), channel_id=1, source_target_pairs={{0,8},{4,12},{8,0},{12,4},{1,9},{5,13},{9,1},{13,5},{2,10},{6,14},... | collective-permute-start | bytes 393224 | tf_op jit(solution)/shard_map/ppermute | solution.py:445

commit v5 on v4

--- a/solution.py
+++ b/solution.py
@@ -368,9 +368,10 @@
     fast = in_range(gauge_ref[0], key_norm, gauge_ref[1])
     copies = [
         pltpu.make_async_copy(
-            out_ref.at[h], out_hbm.at[:, :, lanes_of(g * group_size + h)], sems.at[h]
+            out_ref.at[h, m], out_hbm.at[m, :, lanes_of(g * group_size + h)], sems.at[2 * h + m]
         )
         for h in range(group_size)
+        for m in range(2)
     ]
 
     def scores(m, q):
@@ -387,14 +388,18 @@
         out_ref[h, m] = out.astype(jnp.bfloat16)
 
     def attend(first_half):
+        if not first_half:
+            for h in range(group_size):
+                at = lanes_of(h)
+                out_ref[h, 0] = (acc_ref[0, :, at] / sum_ref[0, :, at]).astype(jnp.bfloat16)
+                copies[2 * h].start()
         for h in range(group_size):
             at, from_q = lanes_of(h), lanes_of(g * group_size + h)
             if first_half:
                 finish(h, 0, at, scores(0, q_ref[0, :, from_q]), shift_ref[0, :, at], None)
-            else:
-                out_ref[h, 0] = (acc_ref[0, :, at] / sum_ref[0, :, at]).astype(jnp.bfloat16)
+                copies[2 * h].start()
             finish(h, 1, at, scores(1, q_ref[1, :, from_q]), shift_ref[1, :, at], None)
-            copies[h].start()
+            copies[2 * h + 1].start()
         for copy in copies:
             copy.wait()
 
@@ -551,7 +556,7 @@
                     pltpu.VMEM((late * rows, HEAD_SIZE), jnp.bfloat16),
                     pltpu.VMEM((late * rows, 2 * HEAD_SIZE), jnp.bfloat16),
                     pltpu.VMEM((group_size, 2, rows, HEAD_SIZE), jnp.bfloat16),
-                    pltpu.SemaphoreType.DMA((group_size,)),
+                    pltpu.SemaphoreType.DMA((2 * group_size,)),
                 ],
                 input_output_aliases={7 + late: 0} if out else {},
                 compiler_params=params,

time: 52.2 us -> 52.2 us (level)
  no operation moved by 1% of the time
where the time goes in v5:
time: 52.2 us; the launch traced here: 52 us
  Pallas kernels  37 us (71%)
  starting transfers between devices  6.71 us (13%)
  local copies, waits for them, and re-layouts  4.79 us (9%)
  waiting for transfers between devices  3.28 us (6%)
    pallas_call x1, Pallas kernels, per_device(): pl.pallas_call(functools.partial(middle_kernel, rows, kv, group_size), ou...  14.6 us
    pallas_call x2, Pallas kernels, per_device(): pl.pallas_call(functools.partial(far_kernel, rows, g, group_size, late),...  13.5 us
    pallas_call x2, Pallas kernels, per_device(): pl.pallas_call(functools.partial(own_kernel, rows, g, group_size), out_sh...  7.01 us
    ppermute x5, starting transfers between devices, shifted(): return lax.ppermute(x, 'ctx', [(i, (i + d) % n) for i in range(n)])  6.71 us
    unnamed x10, local copies, waits for them, and re-layouts  4.79 us
    ppermute x5, waiting for transfers between devices, shifted(): return lax.ppermute(x, 'ctx', [(i, (i + d) % n) for i in range(n)])  3.28 us
    pallas_call x1, Pallas kernels, per_device(): pl.pallas_call(functools.partial(prep_kernel, n, rows, kv), out_shape=[pi...  1.55 us
  transfers between devices with their start and end apart: 5, of which 1 were waited for; matrix products, arithmetic and copies ran while one was open for 0% of the time, Pallas kernels for 58%

profile of v5, /device:TPU:18, one launch (start us, length us, event | category | flops | bytes accessed | tf_op | source)
XLA Modules:
  0.0 52.0 jit_solution(4200345812091427746)
XLA Ops:
  0.0 1.6 %collective-permute-start = (bf16[2,256,256]{2,1,0:T(8,128)(2,1)}, bf16[2,256,256]{2,1,0:T(8,128)(2,1)S(1)}, u32[]{:S(2)}, u32[]{:S(2)}) collective-permute-start(bf16[2,256,256]{2,1,0:T(8,128)(2,1)} %bitcast.8), channel_id=1, source_target_pairs={{0,4},{4,8},{8,12},{12,0},{1,5},{5,9},{9,13},{13,1},{2,6},{6,10},{... | collective-permute-start | bytes 786440 | tf_op jit(solution)/shard_map/ppermute | solution.py:450
  1.6 0.2 collective-permute-start.1
  1.8 0.0 copy-start.1
  1.8 0.9 %copy-done.1 = bf16[1,2,256,256]{3,2,1,0:T(8,128)(2,1)S(1)} copy-done((bf16[1,2,256,256]{3,2,1,0:T(8,128)(2,1)S(1)}, bf16[1,2,256,256]{3,2,1,0:T(8,128)(2,1)}, u32[]{:S(2)}) %copy-start.1) | copy-done | bytes 262168
  2.8 0.0 copy-start.2
  2.8 0.9 %copy-done.2 = bf16[1,2,256,256]{3,2,1,0:T(8,128)(2,1)S(1)} copy-done((bf16[1,2,256,256]{3,2,1,0:T(8,128)(2,1)S(1)}, bf16[1,2,256,256]{3,2,1,0:T(8,128)(2,1)}, u32[]{:S(2)}) %copy-start.2) | copy-done | bytes 262168
  3.7 0.0 copy-start.3
  3.7 0.7 %copy-done.3 = s32[1,2,1024]{2,1,0:T(2,128)S(1)} copy-done((s32[1,2,1024]{2,1,0:T(2,128)S(1)}, s32[1,2,1024]{2,1,0:T(2,128)}, u32[]{:S(2)}) %copy-start.3) | copy-done | bytes 8216
  4.4 1.5 %prep.1 = (bf16[2,256,128]{2,1,0:T(8,128)(2,1)S(1)}, bf16[2,256,128]{2,1,0:T(8,128)(2,1)S(1)}, bf16[2,256,256]{2,1,0:T(8,128)(2,1)S(1)}, f32[2,2,512]{2,1,0:T(2,...) custom-call(s32[1]{0:T(128)} %bitcast.rank_ref.refs_0_, ...), custom_call_target="tpu_custom_call" | custom-call | tf_op jit(solution)/shard_map/prep/pallas_call | solution.py:454
  6.0 1.9 %collective-permute-start.2 = (bf16[2,256,256]{2,1,0:T(8,128)(2,1)S(1)}, bf16[2,256,256]{2,1,0:T(8,128)(2,1)S(1)}, u32[]{:S(2)}, u32[]{:S(2)}) collective-permute-start(bf16[2,256,256]{2,1,0:T(8,128)(2,1)S(1)} %get-tuple-element.34), channel_id=1, source_target_pairs={{0,12},{4,0},{8,4},{12,8},{1,13},{5,1},{9,5},{13,9},{2,14},{6,2},{... | collective-permute-start | bytes 786440 | tf_op jit(solution)/shard_map/ppermute | solution.py:450
  7.8 0.0 copy-start
  7.8 1.5 %copy-done = bf16[1,2,256,1792]{3,2,1,0:T(8,128)(2,1)S(1)} copy-done((bf16[1,2,256,1792]{3,2,1,0:T(8,128)(2,1)S(1)}, bf16[1,2,256,1792]{3,2,1,0:T(8,128)(2,1)}, u32[]{:S(2)}) %copy-start) | copy-done | bytes 1835032
  9.3 0.0 copy-start.4
  9.3 0.7 %copy-done.4 = s32[1,14,64]{2,0,1:T(1,128)S(1)} copy-done((s32[1,14,64]{2,0,1:T(1,128)S(1)}, s32[1,14,64]{2,0,1:T(1,128)}, u32[]{:S(2)}) %copy-start.4) | copy-done | bytes 3608
  10.0 0.4 slash.1
  10.4 3.5 %own.2 = (f32[2,256,896]{2,1,0:T(8,128)S(1)}, f32[2,256,896]{2,1,0:T(8,128)S(1)}, f32[2,256,896]{2,1,0:T(8,128)S(1)}, f32[2,8,128]{2,1,0:T(8,128)S(1)}, f32[7,12...) custom-call(bf16[2,256,1792]{2,1,0:T(8,128)(2,1)S(1)} %get-tuple-element.33.q_ref.refs_1_, ...), custom_call_target="tpu_custom_call" | custom-call | flops 939524096 | bytes 16000000 | tf_op jit(solution)/shard_map/own/pallas_call | solution.py:504
  13.9 2.2 %collective-permute-start.4 = (bf16[2,256,128]{2,1,0:T(8,128)(2,1)S(1)}, bf16[2,256,128]{2,1,0:T(8,128)(2,1)S(1)}, u32[]{:S(2)}, u32[]{:S(2)}) collective-permute-start(bf16[2,256,128]{2,1,0:T(8,128)(2,1)S(1)} %get-tuple-element.60), channel_id=1, source_target_pairs={{0,8},{4,12},{8,0},{12,4},{1,9},{5,13},{9,1},{13,5},{2,10},{6,14},... | collective-permute-start | bytes 393224 | tf_op jit(solution)/shard_map/ppermute | solution.py:450
  16.1 3.5 %own.3 = (f32[2,256,896]{2,1,0:T(8,128)S(1)}, f32[2,256,896]{2,1,0:T(8,128)S(1)}, f32[2,256,896]{2,1,0:T(8,128)S(1)}, f32[2,8,128]{2,1,0:T(8,128)S(1)}, f32[7,12...) custom-call(bf16[2,256,1792]{2,1,0:T(8,128)(2,1)S(1)} %get-tuple-element.33.q_ref.refs_1_, ...), custom_call_target="tpu_custom_call" | custom-call | flops 939524096 | bytes 16000000 | tf_op jit(solution)/shard_map/own/pallas_call | solution.py:504
  19.6 0.9 %collective-permute-start.3 = (bf16[2,256,128]{2,1,0:T(8,128)(2,1)S(1)}, bf16[2,256,128]{2,1,0:T(8,128)(2,1)S(1)}, u32[]{:S(2)}, u32[]{:S(2)}) collective-permute-start(bf16[2,256,128]{2,1,0:T(8,128)(2,1)S(1)} %get-tuple-element.56), channel_id=1, source_target_pairs={{0,8},{4,12},{8,0},{12,4},{1,9},{5,13},{9,1},{13,5},{2,10},{6,14},... | collective-permute-start | bytes 393224 | tf_op jit(solution)/shard_map/ppermute | solution.py:450
  20.4 0.0 collective-permute-done.k_ref
  20.4 3.3 %collective-permute-done.1.v_ref = bf16[2,256,256]{2,1,0:T(8,128)(2,1)S(1)} collective-permute-done((bf16[2,256,256]{2,1,0:T(8,128)(2,1)}, bf16[2,256,256]{2,1,0:T(8,128)(2,1)S(1)}, u32[]{:S(2)}, u32[]{:S(2)}) %collective-permute-start.1) | collective-permute-done | bytes 262176 | tf_op jit(solution)/shard_map/ppermute | solution.py:450
  23.7 0.0 collective-permute-done.2.first_ref
  23.7 14.6 %middle.1 = (f32[2,256,896]{2,1,0:T(8,128)S(1)}, f32[2,256,896]{2,1,0:T(8,128)S(1)}, f32[2,256,896]{2,1,0:T(8,128)S(1)}, f32[2,256,896]{2,1,0:T(8,128)S(1)}, f32...) custom-call(s32[1]{0:T(128)} %bitcast.rank_ref.refs_0_, ...), custom_call_target="tpu_custom_call", output_to_operand_aliasing={{0}: (8, {}), {1}: (9, {}), {2}: (10, {}), {3}: (11, {}), {... | custom-call | flops 2348810240 | bytes 16000000 | tf_op jit(solution)/shard_map/middle/pallas_call | solution.py:529
  38.3 0.0 collective-permute-done.4.refs_7_
  38.3 6.7 %far.2.refs_8_ = bf16[2,256,1792]{2,1,0:T(8,128)(2,1)} custom-call(s32[1]{0:T(128)} %bitcast.rank_ref.refs_0_, bf16[2,256,1792]{2,1,0:T(8,128)(2,1)S(1)} %get-tuple-element.33.q_ref.refs_1_, f32[2,256,896]{2,1,0:T(8,128)S(1)} %get-tuple-element.57.refs_2_, f32[2,256,896]{2,1,0:T(8,128)S(1)} %get-tuple-element.58.refs_3_, ...), custom_call_target="tpu_custom_call" | custom-call | flops 469762048 | bytes 16000000 | tf_op jit(solution)/shard_map/far/pallas_call | solution.py:550
  45.0 0.0 collective-permute-done.3.refs_7_
  45.1 6.7 %far.3 = bf16[2,256,1792]{2,1,0:T(8,128)(2,1)} custom-call(s32[1]{0:T(128)} %bitcast.rank_ref.refs_0_, bf16[2,256,1792]{2,1,0:T(8,128)(2,1)S(1)} %get-tuple-element.33.q_ref.refs_1_, f32[2,256,896]{2,1,0:T(8,128)S(1)} %get-tuple-element.53.refs_2_, f32[2,256,896]{2,1,0:T(8,128)S(1)} %get-tuple-element.54.refs_3_, ...), custom_call_target="tpu_custom_call", output_to_operand_aliasing={{}: (8, {})} | custom-call | flops 469762048 | bytes 16000000 | tf_op jit(solution)/shard_map/far/pallas_call | solution.py:550
Async XLA Ops:
  0.0 20.4 %collective-permute-start = (bf16[2,256,256]{2,1,0:T(8,128)(2,1)}, bf16[2,256,256]{2,1,0:T(8,128)(2,1)S(1)}, u32[]{:S(2)}, u32[]{:S(2)}) collective-permute-start(bf16[2,256,256]{2,1,0:T(8,128)(2,1)} %bitcast.8), channel_id=1, source_target_pairs={{0,4},{4,8},{8,12},{12,0},{1,5},{5,9},{9,13},{13,1},{2,6},{6,10},{... | collective-permute-start | bytes 786440 | tf_op jit(solution)/shard_map/ppermute | solution.py:450
  1.6 22.1 %collective-permute-start.1 = (bf16[2,256,256]{2,1,0:T(8,128)(2,1)}, bf16[2,256,256]{2,1,0:T(8,128)(2,1)S(1)}, u32[]{:S(2)}, u32[]{:S(2)}) collective-permute-start(bf16[2,256,256]{2,1,0:T(8,128)(2,1)} %bitcast.10), channel_id=1, source_target_pairs={{0,4},{4,8},{8,12},{12,0},{1,5},{5,9},{9,13},{13,1},{2,6},{6,10},{... | collective-permute-start | bytes 786440 | tf_op jit(solution)/shard_map/ppermute | solution.py:450
  1.8 0.9 %copy-start.1 = (bf16[1,2,256,256]{3,2,1,0:T(8,128)(2,1)S(1)}, bf16[1,2,256,256]{3,2,1,0:T(8,128)(2,1)}, u32[]{:S(2)}) copy-start(bf16[1,2,256,256]{3,2,1,0:T(8,128)(2,1)} %param.6) | copy-start | bytes 786436
  2.8 0.9 %copy-start.2 = (bf16[1,2,256,256]{3,2,1,0:T(8,128)(2,1)S(1)}, bf16[1,2,256,256]{3,2,1,0:T(8,128)(2,1)}, u32[]{:S(2)}) copy-start(bf16[1,2,256,256]{3,2,1,0:T(8,128)(2,1)} %param.7) | copy-start | bytes 786436
  3.7 0.7 %copy-start.3 = (s32[1,2,1024]{2,1,0:T(2,128)S(1)}, s32[1,2,1024]{2,1,0:T(2,128)}, u32[]{:S(2)}) copy-start(s32[1,2,1024]{2,1,0:T(2,128)} %param.8) | copy-start | bytes 24580
  6.0 17.8 %collective-permute-start.2 = (bf16[2,256,256]{2,1,0:T(8,128)(2,1)S(1)}, bf16[2,256,256]{2,1,0:T(8,128)(2,1)S(1)}, u32[]{:S(2)}, u32[]{:S(2)}) collective-permute-start(bf16[2,256,256]{2,1,0:T(8,128)(2,1)S(1)} %get-tuple-element.34), channel_id=1, source_target_pairs={{0,12},{4,0},{8,4},{12,8},{1,13},{5,1},{9,5},{13,9},{2,14},{6,2},{... | collective-permute-start | bytes 786440 | tf_op jit(solution)/shard_map/ppermute | solution.py:450
  7.8 1.5 %copy-start = (bf16[1,2,256,1792]{3,2,1,0:T(8,128)(2,1)S(1)}, bf16[1,2,256,1792]{3,2,1,0:T(8,128)(2,1)}, u32[]{:S(2)}) copy-start(bf16[1,2,256,1792]{3,2,1,0:T(8,128)(2,1)} %param.5) | copy-start | bytes 5505028
  9.3 0.7 %copy-start.4 = (s32[1,14,64]{2,0,1:T(1,128)S(1)}, s32[1,14,64]{2,0,1:T(1,128)}, u32[]{:S(2)}) copy-start(s32[1,14,64]{2,0,1:T(1,128)} %param.9) | copy-start | bytes 10756
  13.9 24.4 %collective-permute-start.4 = (bf16[2,256,128]{2,1,0:T(8,128)(2,1)S(1)}, bf16[2,256,128]{2,1,0:T(8,128)(2,1)S(1)}, u32[]{:S(2)}, u32[]{:S(2)}) collective-permute-start(bf16[2,256,128]{2,1,0:T(8,128)(2,1)S(1)} %get-tuple-element.60), channel_id=1, source_target_pairs={{0,8},{4,12},{8,0},{12,4},{1,9},{5,13},{9,1},{13,5},{2,10},{6,14},... | collective-permute-start | bytes 393224 | tf_op jit(solution)/shard_map/ppermute | solution.py:450
  19.6 25.5 %collective-permute-start.3 = (bf16[2,256,128]{2,1,0:T(8,128)(2,1)S(1)}, bf16[2,256,128]{2,1,0:T(8,128)(2,1)S(1)}, u32[]{:S(2)}, u32[]{:S(2)}) collective-permute-start(bf16[2,256,128]{2,1,0:T(8,128)(2,1)S(1)} %get-tuple-element.56), channel_id=1, source_target_pairs={{0,8},{4,12},{8,0},{12,4},{1,9},{5,13},{9,1},{13,5},{2,10},{6,14},... | collective-permute-start | bytes 393224 | tf_op jit(solution)/shard_map/ppermute | solution.py:450
